TPU v7x, 32 devices: a whole 2x2x4 slice. The times are simulated.
32 devices in a mesh: row: 4 (over y, core), col: 8 (over z, x).
Axes of the slice: x: 2, y: 2, z: 4, core: 2. Of those that a mesh axis runs over, the one named last changes fastest.
Arguments:
- features: float32 [3072, 128], P(('row', 'col')), may hold values from -1 to 1
- solves: float32 [3072, 64], P(('row', 'col')), may hold values from -48 to 48
- probes: float32 [3072, 64], P(('row', 'col')), may hold values from -48 to 48
Outputs:
- gradient: float32 [3072, 128], P(('row', 'col'))
All inputs are finite; a program needn't handle non-finite values.
Results may differ from a plain program's by a relative error of at most 0.0003.
Values sent between devices are 32-bit elements; how exact they have to be, the bound alone decides.
No kernel may reach another device: no remote copies, remote signals or barrier semaphores. Data moves between devices by JAX's collectives and lax.ppermute only.
A program may use at most 64 MiB of HBM per device.

v0:
```python
import jax
import jax.numpy as jnp
from jax import lax
from jax.sharding import PartitionSpec as P

HIGH = lax.Precision.HIGHEST


def couple(left_x, left_square, left_u, left_v, col_x, col_u, col_v):
    col_square = jnp.sum(col_x * col_x, axis=1)
    inner = jnp.dot(left_x, col_x.T, precision=HIGH, preferred_element_type=jnp.float32)
    distance = left_square[:, None] + col_square[None, :] - 2.0 * inner
    kernel = jnp.exp(-0.5 * distance)
    weight = jnp.dot(left_u, col_v.T, precision=HIGH, preferred_element_type=jnp.float32)
    weight = weight + jnp.dot(left_v, col_u.T, precision=HIGH, preferred_element_type=jnp.float32)
    return kernel * weight


def local(features, solves, probes):
    shard_len = features.shape[0]
    vectors = solves.shape[1]
    n_row = lax.axis_size("row")
    n_col = lax.axis_size("col")
    total = shard_len * n_row * n_col
    rows_x, rows_u, rows_v = (
        lax.all_gather(features, "col", axis=0, tiled=True),
        lax.all_gather(solves, "col", axis=0, tiled=True),
        lax.all_gather(probes, "col", axis=0, tiled=True),
    )
    rows_square = jnp.sum(rows_x * rows_x, axis=1)
    col_x = lax.all_gather(features, "row", axis=0, tiled=True)
    col_u = lax.all_gather(solves, "row", axis=0, tiled=True)
    col_v = lax.all_gather(probes, "row", axis=0, tiled=True)
    coupling = couple(rows_x, rows_square, rows_u, rows_v, col_x, col_u, col_v)
    mixed = jnp.dot(coupling, col_x, precision=HIGH, preferred_element_type=jnp.float32)
    totals = jnp.sum(coupling, axis=1)
    row_mixed = mixed
    row_totals = totals
    mixed, totals = (
        lax.psum_scatter(row_mixed, "col", scatter_dimension=0, tiled=True),
        lax.psum_scatter(row_totals, "col", scatter_dimension=0, tiled=True),
    )
    scale = -2.0 / jnp.sqrt(jnp.float32(total) * jnp.float32(vectors))
    return scale * (features * totals[:, None] - mixed)


def solution(mesh):
    in_specs = (P(("row", "col"), None), P(("row", "col"), None), P(("row", "col"), None))
    out_specs = P(("row", "col"), None)
    return jax.shard_map(local, mesh=mesh, in_specs=in_specs, out_specs=out_specs, check_vma=False)
```

profile of v0, /device:TPU:0, one launch (start us, length us, event | category | flops | bytes accessed | tf_op | source)
XLA Modules:
  0.0 197.2 jit_solution(3642117405220465481)
XLA Ops:
  6.5 0.0 copy-start.1
  6.5 0.0 reduce-scatter.2.cloned.1.call-start
  6.5 7.2 %all_gather.19 = f32[384,128]{1,0:T(8,128)S(1)} all-gather(f32[96,128]{1,0:T(8,128)} %param.3), channel_id=1, replica_groups=mesh['row'=4,'col'=8] {'row'}, dimensions={0}, use_global_device_ids=true | all-gather | bytes 245760 | tf_op jit(solution)/shard_map/all_gather | solution.py:31
  13.7 31.9 %all_gather.18 = f32[768,128]{1,0:T(8,128)S(1)} all-gather(f32[96,128]{1,0:T(8,128)} %param.3), channel_id=1, replica_groups=mesh['row'=4,'col'=8] {'col'}, dimensions={0}, use_global_device_ids=true | all-gather | bytes 442368 | tf_op jit(solution)/shard_map/all_gather | solution.py:26
  45.6 5.6 %all-gather.1 = f32[4,96,64]{1,2,0:T(8,128)S(1)} all-gather(f32[1,96,64]{1,2,0:T(8,128)} %bitcast.19), channel_id=1, replica_groups=mesh['row'=4,'col'=8] {'row'}, dimensions={0}, use_global_device_ids=true | all-gather | bytes 122880 | tf_op jit(solution)/shard_map/all_gather | solution.py:33
  51.3 30.9 %all-gather.2 = f32[8,96,64]{1,2,0:T(8,128)S(1)} all-gather(f32[1,96,64]{1,2,0:T(8,128)} %bitcast.20), channel_id=1, replica_groups=mesh['row'=4,'col'=8] {'col'}, dimensions={0}, use_global_device_ids=true | all-gather | bytes 221184 | tf_op jit(solution)/shard_map/all_gather | solution.py:28
  82.2 30.9 %all-gather = f32[8,96,64]{1,2,0:T(8,128)S(1)} all-gather(f32[1,96,64]{1,2,0:T(8,128)} %bitcast.21), channel_id=1, replica_groups=mesh['row'=4,'col'=8] {'col'}, dimensions={0}, use_global_device_ids=true | all-gather | bytes 221184 | tf_op jit(solution)/shard_map/all_gather | solution.py:27
  113.1 0.0 copy-done.1
  113.2 5.4 %all-gather.3 = f32[4,96,64]{1,2,0:T(8,128)S(1)} all-gather(f32[1,96,64]{1,2,0:T(8,128)S(1)} %bitcast.22), channel_id=1, replica_groups=mesh['row'=4,'col'=8] {'row'}, dimensions={0}, use_global_device_ids=true | all-gather | bytes 122880 | tf_op jit(solution)/shard_map/all_gather | solution.py:32
  118.6 0.1 multiply_reduce_fusion.1
  118.7 0.2 multiply_reduce_fusion
  118.9 0.2 copy.8
  119.1 0.1 reshape.4
  119.2 0.1 copy.9
  119.3 0.1 reshape.6
  119.4 0.2 copy.10
  119.6 0.1 reshape.8
  119.7 0.1 copy.11
  119.8 0.1 reshape.10
  119.9 1.3 fusion.3
  121.2 1.1 fusion.5
  122.3 1.2 fusion.4
  123.5 0.0 copy-start.2
  123.5 0.0 copy-start
  123.5 2.8 %fusion.6 = f32[768,128]{1,0:T(8,128)} fusion(f32[768,384]{0,1:T(8,128)S(1)} %get-tuple-element.6, f32[384,128]{1,0:T(8,128)S(1)} %all_gather.19), kind=kOutput, calls=%fused_computation.11 | convolution fusion | flops 452984832 | bytes 1769472 | tf_op jit(solution)/shard_map/dot_general | solution.py:35
  126.3 0.0 reduce-scatter.2.cloned.1.call-update
  126.3 0.0 copy-done.2
  126.3 0.6 dynamic-slice
  127.6 21.4 %all-reduce = f32[768]{0:T(1024)S(1)} all-reduce(f32[768]{0:T(1024)S(1)} %get-tuple-element.5), channel_id=2, replica_groups=mesh['row'=4,'col'=8] {'col'}, use_global_device_ids=true, to_apply=%region_3.0.clone | all-reduce | flops 768 | bytes 6144
  149.0 0.1 dynamic-slice.1
  149.1 39.7 %reduce-scatter.2.cloned.1.call-done = f32[96,128]{1,0:T(8,128)} async-done(((f32[768,128]{1,0:T(8,128)}), f32[96,128]{1,0:T(8,128)}) %reduce-scatter.2.cloned.1.call-update) | async-done | bytes 49168 | tf_op jit(solution)/shard_map/reduce_scatter | solution.py:40
  188.8 0.0 copy-done
  188.8 1.5 subtract_multiply_fusion
Async XLA Ops:
  6.5 106.6 %copy-start.1 = (f32[96,64]{0,1:T(8,128)S(1)}, f32[96,64]{0,1:T(8,128)}, u32[]{:S(2)}) copy-start(f32[96,64]{0,1:T(8,128)} %param.4) | copy-start | bytes 73732
  6.5 182.3 %reduce-scatter.2.cloned.1.call-start = ((), (), s32[]{:S(2)}) async-start(), calls=%async_computation.1 | async-start | bytes 442368 | tf_op jit(solution)/shard_map/reduce_scatter | solution.py:40
  123.5 2.9 %copy-start.2 = (u32[32]{0:T(128)S(1)}, u32[32]{0:T(128)}, u32[]{:S(2)}) copy-start(u32[32]{0:T(128)} %constant.10) | copy-start | bytes 388
  123.5 65.3 %copy-start = (f32[96,128]{1,0:T(8,128)S(1)}, f32[96,128]{1,0:T(8,128)}, u32[]{:S(2)}) copy-start(f32[96,128]{1,0:T(8,128)} %param.3) | copy-start | bytes 147460
Sparse Core Ops, SparseCore 0:
  126.4 62.3 reduce-scatter.1
where the time goes:
time: 197 us
  blocking collectives  133 us (68%)
  waiting for transfers between devices  39.8 us (20%)
  between operations  14.1 us (7%)
  matrix products  6.34 us (3%)
    reduce_scatter x1, waiting for transfers between devices, local(): lax.psum_scatter(row_mixed, 'col', scatter_dimension=0, tiled=True)  39.7 us
    all_gather x1, blocking collectives, local(): lax.all_gather(features, 'col', axis=0, tiled=True)  31.9 us
    all_gather x1, blocking collectives, local(): lax.all_gather(probes, 'col', axis=0, tiled=True)  30.9 us
    all_gather x1, blocking collectives, local(): lax.all_gather(solves, 'col', axis=0, tiled=True)  30.9 us
    unnamed x1, blocking collectives  21.4 us
    all_gather x1, blocking collectives, local(): col_x = lax.all_gather(features, 'row', axis=0, tiled=True)  7.19 us
    all_gather x1, blocking collectives, local(): col_v = lax.all_gather(probes, 'row', axis=0, tiled=True)  5.62 us
    all_gather x1, blocking collectives, local(): col_u = lax.all_gather(solves, 'row', axis=0, tiled=True)  5.41 us
  transfers between devices with their start and end apart: 1, of which 1 were waited for; matrix products, arithmetic and copies ran while one was open for 0% of the time, Pallas kernels for 0%

commit v1 on v0

v1 whole, which is shorter than its diff:
```python
import functools

import jax
import jax.numpy as jnp
from jax import lax
from jax.experimental import pallas as pl
from jax.experimental.pallas import tpu as pltpu
from jax.sharding import Mesh, PartitionSpec as P

NT = (((1,), (1,)), ((), ()))
NN = (((1,), (0,)), ((), ()))


def shifted(index, step, size):
    return index ^ step if size & (size - 1) == 0 else (index + step) % size


def send(block, axis, step, back=False):
    size = lax.axis_size(axis)
    pairs = [(i, shifted(i, step, size)) for i in range(size)]
    return lax.ppermute(block, axis, [(j, i) for i, j in pairs] if back else pairs)


def pieces(value, count):
    parts = []
    for _ in range(count):
        part = value.astype(jnp.bfloat16)
        parts.append(part)
        value = value - part.astype(jnp.float32)
    return parts


def product(left, right, dims):
    count = len(left)
    total = None
    for order in range(count - 1, -1, -1):
        for i in range(order + 1):
            term = lax.dot_general(left[i], right[order - i], dims, preferred_element_type=jnp.float32)
            total = term if total is None else total + term
    return total


def couple(features, scale, n_targets, n_sources, n_sums, *refs):
    targets = refs[:n_targets]
    sources = refs[n_targets : n_targets + n_sources]
    sums = refs[n_targets + n_sources : n_targets + n_sources + n_sums]
    outs = refs[n_targets + n_sources + n_sums :]
    source = jnp.concatenate([ref[...] for ref in sources], axis=0)
    xs, ws = source[:, :features], source[:, features:]
    half = ws.shape[1] // 2
    ws = jnp.concatenate([ws[:, half:], ws[:, :half]], axis=1)
    xs_pieces, ws_pieces = pieces(xs, 3), pieces(ws, 2)
    ones = jnp.ones((8, features), jnp.bfloat16)
    square_s = sum(lax.dot_general(ones, part, NT, preferred_element_type=jnp.float32) for part in reversed(pieces(xs * xs, 3)))[:1]
    group = n_targets // len(outs)
    for g, out in enumerate(outs):
        target = jnp.concatenate([ref[...] for ref in targets[g * group : (g + 1) * group]], axis=0)
        xt, wt = target[:, :features], target[:, features:]
        inner = product(pieces(xt, 3), xs_pieces, NT)
        dist = jnp.sum(xt * xt, axis=1, keepdims=True) + square_s - 2.0 * inner
        coupling = jnp.exp(-0.5 * dist) * product(pieces(wt, 2), ws_pieces, NT)
        totals = jnp.sum(coupling, axis=1, keepdims=True)
        mixed = product(pieces(coupling, 2), xs_pieces[:2], NN)
        value = scale * (xt * totals - mixed)
        out[...] = value + sums[g][...] if n_sums else value


def partial(features, scale, groups, sources, sums):
    targets = [block for group in groups for block in group]
    rows, width = targets[0].shape
    n_t, n_s = rows * len(targets), rows * len(sources)
    return pl.pallas_call(
        functools.partial(couple, features, scale, len(targets), len(sources), len(sums)),
        out_shape=[jax.ShapeDtypeStruct((rows * len(group), features), jnp.float32) for group in groups],
        in_specs=[pl.BlockSpec(memory_space=pltpu.VMEM)] * (len(targets) + len(sources) + len(sums)),
        out_specs=[pl.BlockSpec(memory_space=pltpu.VMEM)] * len(groups),
        cost_estimate=pl.CostEstimate(
            flops=24 * n_t * n_s * features, bytes_accessed=4 * (n_t + n_s) * width, transcendentals=n_t * n_s
        ),
        compiler_params=pltpu.CompilerParams(vmem_limit_bytes=48 * 1024 * 1024),
    )(*targets, *sources, *sums)


def local(total, features, solves, probes):
    width, vectors = features.shape[1], solves.shape[1]
    scale = -2.0 / (float(total) * float(vectors)) ** 0.5
    n_far, n_x, n_y = lax.axis_size("far"), lax.axis_size("x"), lax.axis_size("y")
    n_core = lax.axis_size("core")
    own = jnp.concatenate([features, solves, probes], axis=1)
    rows = own.shape[0]

    far = {step: send(own, "far", step) for step in range(n_far - 1, 0, -1)}
    beside = [own] + [send(own, "x", step) for step in range(1, n_x)]
    pair = jnp.concatenate(beside, axis=0)
    groups = [beside]
    for step in range(1, n_y):
        block = send(pair, "y", step)
        groups.append([block[i * rows : (i + 1) * rows] for i in range(n_x)])
    groups = [[groups[y][x] for y in range(n_y)] for x in range(n_x)]

    sums = []
    near = [own] + [send(own, "core", step) for step in range(1, n_core)]
    sums = partial(width, scale, groups, near, sums)
    for step in range(1, n_far):
        block = far[step]
        sources = [block] + [send(block, "core", other) for other in range(1, n_core)]
        sums = partial(width, scale, groups, sources, sums)

    column = sums[0]
    for step in range(1, n_x):
        column = column + send(sums[step], "x", step, back=True)
    out = column[:rows]
    for step in range(1, n_y):
        out = out + send(column[step * rows : (step + 1) * rows], "y", step, back=True)
    return out


def solution(mesh):
    n_row, n_col = mesh.shape["row"], mesh.shape["col"]
    n_core, n_x = (2 if n % 2 == 0 else 1 for n in (n_row, n_col))
    shape = (n_row // n_core, n_core, n_col // n_x, n_x)
    fine = Mesh(mesh.devices.reshape(shape), ("y", "core", "far", "x"))
    spec = P(("y", "core", "far", "x"), None)

    def run(features, solves, probes):
        inner = functools.partial(local, features.shape[0])
        return jax.shard_map(inner, mesh=fine, in_specs=(spec,) * 3, out_specs=spec, check_vma=False)(features, solves, probes)

    return run
```

time: 197 us -> 35.2 us (0.18)
  blocking collectives: 133 us -> 0 us
  waiting for transfers between devices: 39.8 us -> 16.4 us
  between operations: 14.1 us -> 0.11 us
  starting transfers between devices: 0.01 us -> 11.4 us
  matrix products: 6.34 us -> 0 us
  Pallas kernels: 0 us -> 4.62 us
    all_gather x6 -> x0, blocking collectives: 112 us -> none  [the longest x1 31.9 us: local(): lax.all_gather(features, 'col', axis=0, tiled=True)]
    reduce_scatter x1 -> x0, waiting for transfers between devices: 39.7 us -> none  [local(): lax.psum_scatter(row_mixed, 'col', scatter_dimension=0, tiled=True)]
    unnamed x1 -> x0, blocking collectives: 21.4 us -> none
    ppermute x0 -> x11, waiting for transfers between devices: none -> 16.4 us  [send(): lax.ppermute(block, axis, [(j, i) for i, j in pairs] if back else pairs)]
    ppermute x0 -> x11, starting transfers between devices: none -> 11.4 us  [send(): lax.ppermute(block, axis, [(j, i) for i, j in pairs] if back else pairs)]
    dot_general x4 -> x0, matrix products: 6.34 us -> none  [the longest x1 2.8 us: local(): jnp.dot(coupling, col_x, precision=HIGH, preferred_element_type=jnp.float32)]
    pallas_call x0 -> x4, Pallas kernels: none -> 4.62 us  [partial(): pl.pallas_call(functools.partial(couple, features, scale, len(targets), l...]
  transfers between devices with their start and end apart: 1 -> 11, of which waited for: 1 -> 6; matrix products, arithmetic and copies ran while one was open for 0% -> 0% of each run, Pallas kernels for 0% -> 10%
where the time goes in v1:
time: 35.2 us; the launch traced here: 35 us
  waiting for transfers between devices  16.4 us (47%)
  starting transfers between devices  11.4 us (32%)
  Pallas kernels  4.62 us (13%)
  local copies, waits for them, and re-layouts  1.66 us (5%)
  other arithmetic  0.8 us (2%)
    ppermute x11, waiting for transfers between devices, send(): lax.ppermute(block, axis, [(j, i) for i, j in pairs] if back else pairs)  16.4 us
    ppermute x11, starting transfers between devices, send(): lax.ppermute(block, axis, [(j, i) for i, j in pairs] if back else pairs)  11.4 us
    pallas_call x4, Pallas kernels, partial(): pl.pallas_call(functools.partial(couple, features, scale, len(targets), l...  4.62 us
    unnamed x6, local copies, waits for them, and re-layouts  1.64 us
  transfers between devices with their start and end apart: 11, of which 6 were waited for; matrix products, arithmetic and copies ran while one was open for 0% of the time, Pallas kernels for 10%

profile of v1, /device:TPU:0, one launch (start us, length us, event | category | flops | bytes accessed | tf_op | source)
XLA Modules:
  0.0 35.0 jit_solution(17912696343306485759)
XLA Ops:
  0.0 0.0 copy-start.1
  0.0 0.8 %copy.4 = f32[96,64]{1,0:T(8,128)S(1)} copy(f32[96,64]{0,1:T(8,128)} %param.4) | data formatting | bytes 49152 | tf_op args[1]
  0.9 0.0 copy-done.1
  0.9 0.0 copy-start
  0.9 0.1 copy.5
  1.0 0.7 %copy-done = f32[96,128]{1,0:T(8,128)S(1)} copy-done((f32[96,128]{1,0:T(8,128)S(1)}, f32[96,128]{1,0:T(8,128)}, u32[]{:S(2)}) %copy-start) | copy-done | bytes 49176
  1.7 0.1 pad_maximum_fusion.1.refs_0_.refs_4_
  1.7 3.0 %collective-permute-start = (f32[96,256]{1,0:T(8,128)S(1)}, f32[96,256]{1,0:T(8,128)S(1)}, u32[]{:S(2)}, u32[]{:S(2)}) collective-permute-start(f32[96,256]{1,0:T(8,128)S(1)} %pad_maximum_fusion.1.refs_0_.refs_4_), channel_id=1, source_target_pairs={{0,1},{1,0},{2,3},{3,2},{4,5},{5,4},{6,7},{7,6},{8,9},{9,8},{10,11... | collective-permute-start | bytes 294920 | tf_op jit(solution)/shard_map/ppermute | solution.py:21
  4.7 2.8 %collective-permute-done.refs_2_ = f32[96,256]{1,0:T(8,128)S(1)} collective-permute-done((f32[96,256]{1,0:T(8,128)S(1)}, f32[96,256]{1,0:T(8,128)S(1)}, u32[]{:S(2)}, u32[]{:S(2)}) %collective-permute-start) | collective-permute-done | bytes 98336 | tf_op jit(solution)/shard_map/ppermute | solution.py:21
  7.5 0.1 pad_maximum_fusion
  7.6 1.9 %collective-permute-start.1 = (f32[192,256]{1,0:T(8,128)S(1)}, f32[192,256]{1,0:T(8,128)S(1)}, u32[]{:S(2)}, u32[]{:S(2)}) collective-permute-start(f32[192,256]{1,0:T(8,128)S(1)} %pad_maximum_fusion), channel_id=1, source_target_pairs={{0,16},{16,0},{1,17},{17,1},{2,18},{18,2},{3,19},{19,3},{4,20},{20... | collective-permute-start | bytes 589832 | tf_op jit(solution)/shard_map/ppermute | solution.py:21
  9.5 1.6 %collective-permute-start.6 = (f32[96,256]{1,0:T(8,128)S(1)}, f32[96,256]{1,0:T(8,128)S(1)}, u32[]{:S(2)}, u32[]{:S(2)}) collective-permute-start(f32[96,256]{1,0:T(8,128)S(1)} %pad_maximum_fusion.1.refs_0_.refs_4_), channel_id=1, source_target_pairs={{0,2},{2,0},{4,6},{6,4},{1,3},{3,1},{5,7},{7,5},{8,10},{10,8},{12,... | collective-permute-start | bytes 294920 | tf_op jit(solution)/shard_map/ppermute | solution.py:21
  11.1 2.6 %collective-permute-start.4 = (f32[96,256]{1,0:T(8,128)S(1)}, f32[96,256]{1,0:T(8,128)S(1)}, u32[]{:S(2)}, u32[]{:S(2)}) collective-permute-start(f32[96,256]{1,0:T(8,128)S(1)} %pad_maximum_fusion.1.refs_0_.refs_4_), channel_id=1, source_target_pairs={{0,4},{2,6},{4,0},{6,2},{1,5},{3,7},{5,1},{7,3},{8,12},{10,14},{12... | collective-permute-start | bytes 294920 | tf_op jit(solution)/shard_map/ppermute | solution.py:21
  13.7 0.2 collective-permute-start.2
  13.9 0.0 collective-permute-start.8
  13.9 0.8 %collective-permute-done.6.refs_4_ = f32[96,256]{1,0:T(8,128)S(1)} collective-permute-done((f32[96,256]{1,0:T(8,128)S(1)}, f32[96,256]{1,0:T(8,128)S(1)}, u32[]{:S(2)}, u32[]{:S(2)}) %collective-permute-start.6) | collective-permute-done | bytes 98336 | tf_op jit(solution)/shard_map/ppermute | solution.py:21
  14.8 0.0 collective-permute-start.7
  14.8 4.3 %collective-permute-done.4.refs_4_ = f32[96,256]{1,0:T(8,128)S(1)} collective-permute-done((f32[96,256]{1,0:T(8,128)S(1)}, f32[96,256]{1,0:T(8,128)S(1)}, u32[]{:S(2)}, u32[]{:S(2)}) %collective-permute-start.4) | collective-permute-done | bytes 98336 | tf_op jit(solution)/shard_map/ppermute | solution.py:21
  19.1 0.0 collective-permute-start.5
  19.1 1.2 %collective-permute-done.2.refs_4_ = f32[96,256]{1,0:T(8,128)S(1)} collective-permute-done((f32[96,256]{1,0:T(8,128)S(1)}, f32[96,256]{1,0:T(8,128)S(1)}, u32[]{:S(2)}, u32[]{:S(2)}) %collective-permute-start.2) | collective-permute-done | bytes 98336 | tf_op jit(solution)/shard_map/ppermute | solution.py:21
  20.2 0.0 collective-permute-start.3
  20.2 0.0 collective-permute-done.1
  20.3 0.0 collective-permute-done.8.refs_5_
  20.3 1.2 %shard_map.37 = (f32[192,128]{1,0:T(8,128)S(1)}, f32[192,128]{1,0:T(8,128)S(1)}) custom-call(f32[96,256]{1,0:T(8,128)S(1)} %pad_maximum_fusion.1.refs_0_.refs_4_, f32[96,256]{1,0:T(8,128)S(1)} %get-tuple-element.22.refs_1_, f32[96,256]{1,0:T(8,128)S(1)} %collective-permute-done.refs_2_, f32[96,256]{1,0:T(8,128)S(1)} %get-tuple-element.21.refs_3_, ...), custom_call_target="tpu_custom_call" | custom-call | flops 226492416 | bytes 589824 | tf_op jit(solution)/shard_map/pallas_call | solution.py:72
  21.4 0.0 collective-permute-done.7.refs_5_
  21.4 1.2 %shard_map.38 = (f32[192,128]{1,0:T(8,128)S(1)}, f32[192,128]{1,0:T(8,128)S(1)}) custom-call(f32[96,256]{1,0:T(8,128)S(1)} %pad_maximum_fusion.1.refs_0_.refs_4_, f32[96,256]{1,0:T(8,128)S(1)} %get-tuple-element.22.refs_1_, f32[96,256]{1,0:T(8,128)S(1)} %collective-permute-done.refs_2_, f32[96,256]{1,0:T(8,128)S(1)} %get-tuple-element.21.refs_3_, ...), custom_call_target="tpu_custom_call" | custom-call | flops 226492416 | bytes 589824 | tf_op jit(solution)/shard_map/pallas_call | solution.py:72
  22.6 0.0 collective-permute-done.5.refs_5_
  22.6 1.2 %shard_map.39 = (f32[192,128]{1,0:T(8,128)S(1)}, f32[192,128]{1,0:T(8,128)S(1)}) custom-call(f32[96,256]{1,0:T(8,128)S(1)} %pad_maximum_fusion.1.refs_0_.refs_4_, f32[96,256]{1,0:T(8,128)S(1)} %get-tuple-element.22.refs_1_, f32[96,256]{1,0:T(8,128)S(1)} %collective-permute-done.refs_2_, f32[96,256]{1,0:T(8,128)S(1)} %get-tuple-element.21.refs_3_, ...), custom_call_target="tpu_custom_call" | custom-call | flops 226492416 | bytes 589824 | tf_op jit(solution)/shard_map/pallas_call | solution.py:72
  23.8 0.0 collective-permute-done.3.refs_5_
  23.8 1.2 %shard_map.40 = (f32[192,128]{1,0:T(8,128)S(1)}, f32[192,128]{1,0:T(8,128)S(1)}) custom-call(f32[96,256]{1,0:T(8,128)S(1)} %pad_maximum_fusion.1.refs_0_.refs_4_, f32[96,256]{1,0:T(8,128)S(1)} %get-tuple-element.22.refs_1_, f32[96,256]{1,0:T(8,128)S(1)} %collective-permute-done.refs_2_, f32[96,256]{1,0:T(8,128)S(1)} %get-tuple-element.21.refs_3_, ...), custom_call_target="tpu_custom_call" | custom-call | flops 226492416 | bytes 589824 | tf_op jit(solution)/shard_map/pallas_call | solution.py:72
  24.9 1.6 %collective-permute-start.9 = (f32[192,128]{1,0:T(8,128)S(1)}, f32[192,128]{1,0:T(8,128)S(1)}, u32[]{:S(2)}, u32[]{:S(2)}) collective-permute-start(f32[192,128]{1,0:T(8,128)S(1)} %get-tuple-element.20), channel_id=1, source_target_pairs={{1,0},{0,1},{3,2},{2,3},{5,4},{4,5},{7,6},{6,7},{9,8},{8,9},{11,10... | collective-permute-start | bytes 294920 | tf_op jit(solution)/shard_map/ppermute | solution.py:21
  26.5 3.7 %collective-permute-done.9 = f32[192,128]{1,0:T(8,128)S(1)} collective-permute-done((f32[192,128]{1,0:T(8,128)S(1)}, f32[192,128]{1,0:T(8,128)S(1)}, u32[]{:S(2)}, u32[]{:S(2)}) %collective-permute-start.9) | collective-permute-done | bytes 98336 | tf_op jit(solution)/shard_map/ppermute | solution.py:21
  30.2 0.6 %collective-permute-start.10 = (f32[96,128]{1,0:T(8,128)S(1)}, f32[96,128]{1,0:T(8,128)S(1)}, u32[]{:S(2)}, u32[]{:S(2)}) collective-permute-start(f32[96,128]{1,0:T(8,128)S(1)} %slice.19), channel_id=1, source_target_pairs={{16,0},{0,16},{17,1},{1,17},{18,2},{2,18},{19,3},{3,19},{20,4},{4,... | collective-permute-start | bytes 147464 | tf_op jit(solution)/shard_map/ppermute | solution.py:21
  30.8 3.6 %collective-permute-done.10 = f32[96,128]{1,0:T(8,128)S(1)} collective-permute-done((f32[96,128]{1,0:T(8,128)S(1)}, f32[96,128]{1,0:T(8,128)S(1)}, u32[]{:S(2)}, u32[]{:S(2)}) %collective-permute-start.10) | collective-permute-done | bytes 49184 | tf_op jit(solution)/shard_map/ppermute | solution.py:21
  34.4 0.6 %slice_add_fusion = f32[96,128]{1,0:T(8,128)} fusion(f32[96,128]{1,0:T(8,128)S(1)} %collective-permute-done.10, f32[192,128]{1,0:T(8,128)S(1)} %add.6), kind=kLoop, calls=%fused_computation.2 | loop fusion | flops 12288 | bytes 147456 | tf_op jit(solution)/shard_map/add | solution.py:114
  (3 shorter events, 0.0 us)
Async XLA Ops:
  0.0 0.9 %copy-start.1 = (f32[96,64]{0,1:T(8,128)S(1)}, f32[96,64]{0,1:T(8,128)}, u32[]{:S(2)}) copy-start(f32[96,64]{0,1:T(8,128)} %param.5) | copy-start | bytes 73732
  0.9 0.8 %copy-start = (f32[96,128]{1,0:T(8,128)S(1)}, f32[96,128]{1,0:T(8,128)}, u32[]{:S(2)}) copy-start(f32[96,128]{1,0:T(8,128)} %param.3) | copy-start | bytes 147460
  1.7 5.8 %collective-permute-start = (f32[96,256]{1,0:T(8,128)S(1)}, f32[96,256]{1,0:T(8,128)S(1)}, u32[]{:S(2)}, u32[]{:S(2)}) collective-permute-start(f32[96,256]{1,0:T(8,128)S(1)} %pad_maximum_fusion.1.refs_0_.refs_4_), channel_id=1, source_target_pairs={{0,1},{1,0},{2,3},{3,2},{4,5},{5,4},{6,7},{7,6},{8,9},{9,8},{10,11... | collective-permute-start | bytes 294920 | tf_op jit(solution)/shard_map/ppermute | solution.py:21
  7.6 12.6 %collective-permute-start.1 = (f32[192,256]{1,0:T(8,128)S(1)}, f32[192,256]{1,0:T(8,128)S(1)}, u32[]{:S(2)}, u32[]{:S(2)}) collective-permute-start(f32[192,256]{1,0:T(8,128)S(1)} %pad_maximum_fusion), channel_id=1, source_target_pairs={{0,16},{16,0},{1,17},{17,1},{2,18},{18,2},{3,19},{19,3},{4,20},{20... | collective-permute-start | bytes 589832 | tf_op jit(solution)/shard_map/ppermute | solution.py:21
  9.5 5.2 %collective-permute-start.6 = (f32[96,256]{1,0:T(8,128)S(1)}, f32[96,256]{1,0:T(8,128)S(1)}, u32[]{:S(2)}, u32[]{:S(2)}) collective-permute-start(f32[96,256]{1,0:T(8,128)S(1)} %pad_maximum_fusion.1.refs_0_.refs_4_), channel_id=1, source_target_pairs={{0,2},{2,0},{4,6},{6,4},{1,3},{3,1},{5,7},{7,5},{8,10},{10,8},{12,... | collective-permute-start | bytes 294920 | tf_op jit(solution)/shard_map/ppermute | solution.py:21
  11.1 7.9 %collective-permute-start.4 = (f32[96,256]{1,0:T(8,128)S(1)}, f32[96,256]{1,0:T(8,128)S(1)}, u32[]{:S(2)}, u32[]{:S(2)}) collective-permute-start(f32[96,256]{1,0:T(8,128)S(1)} %pad_maximum_fusion.1.refs_0_.refs_4_), channel_id=1, source_target_pairs={{0,4},{2,6},{4,0},{6,2},{1,5},{3,7},{5,1},{7,3},{8,12},{10,14},{12... | collective-permute-start | bytes 294920 | tf_op jit(solution)/shard_map/ppermute | solution.py:21
  13.7 6.5 %collective-permute-start.2 = (f32[96,256]{1,0:T(8,128)S(1)}, f32[96,256]{1,0:T(8,128)S(1)}, u32[]{:S(2)}, u32[]{:S(2)}) collective-permute-start(f32[96,256]{1,0:T(8,128)S(1)} %pad_maximum_fusion.1.refs_0_.refs_4_), channel_id=1, source_target_pairs={{0,6},{2,4},{4,2},{6,0},{1,7},{3,5},{5,3},{7,1},{8,14},{10,12},{12... | collective-permute-start | bytes 294920 | tf_op jit(solution)/shard_map/ppermute | solution.py:21
  13.9 6.3 %collective-permute-start.8 = (f32[96,256]{1,0:T(8,128)S(1)}, f32[96,256]{1,0:T(8,128)S(1)}, u32[]{:S(2)}, u32[]{:S(2)}) collective-permute-start(f32[96,256]{1,0:T(8,128)S(1)} %pad_maximum_fusion.1.refs_0_.refs_4_), channel_id=1, source_target_pairs={{0,8},{8,0},{1,9},{9,1},{2,10},{10,2},{3,11},{11,3},{4,12},{12,4},... | collective-permute-start | bytes 294920 | tf_op jit(solution)/shard_map/ppermute | solution.py:21
  14.8 6.7 %collective-permute-start.7 = (f32[96,256]{1,0:T(8,128)S(1)}, f32[96,256]{1,0:T(8,128)S(1)}, u32[]{:S(2)}, u32[]{:S(2)}) collective-permute-start(f32[96,256]{1,0:T(8,128)S(1)} %collective-permute-done.6.refs_4_), channel_id=1, source_target_pairs={{0,8},{8,0},{1,9},{9,1},{2,10},{10,2},{3,11},{11,3},{4,12},{12,4},... | collective-permute-start | bytes 294920 | tf_op jit(solution)/shard_map/ppermute | solution.py:21
  19.1 3.5 %collective-permute-start.5 = (f32[96,256]{1,0:T(8,128)S(1)}, f32[96,256]{1,0:T(8,128)S(1)}, u32[]{:S(2)}, u32[]{:S(2)}) collective-permute-start(f32[96,256]{1,0:T(8,128)S(1)} %collective-permute-done.4.refs_4_), channel_id=1, source_target_pairs={{0,8},{8,0},{1,9},{9,1},{2,10},{10,2},{3,11},{11,3},{4,12},{12,4},... | collective-permute-start | bytes 294920 | tf_op jit(solution)/shard_map/ppermute | solution.py:21
  20.2 3.5 %collective-permute-start.3 = (f32[96,256]{1,0:T(8,128)S(1)}, f32[96,256]{1,0:T(8,128)S(1)}, u32[]{:S(2)}, u32[]{:S(2)}) collective-permute-start(f32[96,256]{1,0:T(8,128)S(1)} %collective-permute-done.2.refs_4_), channel_id=1, source_target_pairs={{0,8},{8,0},{1,9},{9,1},{2,10},{10,2},{3,11},{11,3},{4,12},{12,4},... | collective-permute-start | bytes 294920 | tf_op jit(solution)/shard_map/ppermute | solution.py:21
  24.9 5.3 %collective-permute-start.9 = (f32[192,128]{1,0:T(8,128)S(1)}, f32[192,128]{1,0:T(8,128)S(1)}, u32[]{:S(2)}, u32[]{:S(2)}) collective-permute-start(f32[192,128]{1,0:T(8,128)S(1)} %get-tuple-element.20), channel_id=1, source_target_pairs={{1,0},{0,1},{3,2},{2,3},{5,4},{4,5},{7,6},{6,7},{9,8},{8,9},{11,10... | collective-permute-start | bytes 294920 | tf_op jit(solution)/shard_map/ppermute | solution.py:21
  30.2 4.2 %collective-permute-start.10 = (f32[96,128]{1,0:T(8,128)S(1)}, f32[96,128]{1,0:T(8,128)S(1)}, u32[]{:S(2)}, u32[]{:S(2)}) collective-permute-start(f32[96,128]{1,0:T(8,128)S(1)} %slice.19), channel_id=1, source_target_pairs={{16,0},{0,16},{17,1},{1,17},{18,2},{2,18},{19,3},{3,19},{20,4},{4,... | collective-permute-start | bytes 147464 | tf_op jit(solution)/shard_map/ppermute | solution.py:21

commit v2 on v1

v2 whole, which is shorter than its diff:
```python
import functools
import itertools

import jax
import jax.numpy as jnp
from jax import lax
from jax.experimental import pallas as pl
from jax.experimental.pallas import tpu as pltpu
from jax.sharding import Mesh, PartitionSpec as P

NT = (((1,), (1,)), ((), ()))
NN = (((1,), (0,)), ((), ()))


def shifted(index, step, size):
    return index ^ step if size & (size - 1) == 0 else (index + step) % size


def send(block, axes, steps, back=False):
    sizes = [lax.axis_size(axis) for axis in axes]
    places = list(itertools.product(*map(range, sizes)))
    number = {place: i for i, place in enumerate(places)}
    pairs = [(number[place], number[tuple(map(shifted, place, steps, sizes))]) for place in places]
    return lax.ppermute(block, axes, [(j, i) for i, j in pairs] if back else pairs)


def pieces(value, count):
    parts = []
    for _ in range(count):
        part = value.astype(jnp.bfloat16)
        parts.append(part)
        value = value - part.astype(jnp.float32)
    return parts


def product(left, right, dims):
    terms = [(left[i], right[order - i]) for order in range(len(left)) for i in range(order + 1)]
    long_left, long_right = (jnp.concatenate(side, axis=axis[0]) for side, axis in zip(zip(*terms), dims[0]))
    return lax.dot_general(long_left, long_right, dims, preferred_element_type=jnp.float32)


def pack(features_ref, solves_ref, probes_ref, out_ref, both, sems):
    width, vectors = features_ref.shape[1], solves_ref.shape[0]
    copies = [
        pltpu.make_async_copy(solves_ref, both.at[:vectors], sems.at[0]),
        pltpu.make_async_copy(probes_ref, both.at[vectors:], sems.at[1]),
        pltpu.make_async_copy(features_ref, out_ref.at[:, :width], sems.at[2]),
    ]
    for copy in copies:
        copy.start()
    for copy in copies[:2]:
        copy.wait()
    out_ref[:, width:] = both[...].T
    copies[2].wait()


def packed(features, solves, probes):
    rows, width = features.shape[0], features.shape[1] + solves.shape[1] + probes.shape[1]
    return pl.pallas_call(
        pack,
        out_shape=pltpu.VMEM((rows, width), jnp.float32),
        in_specs=[pl.BlockSpec(memory_space=pltpu.HBM)] * 3,
        out_specs=pl.BlockSpec(memory_space=pltpu.VMEM),
        scratch_shapes=[
            pltpu.VMEM((solves.shape[1] + probes.shape[1], rows), jnp.float32),
            pltpu.SemaphoreType.DMA((3,)),
        ],
        compiler_params=pltpu.CompilerParams(vmem_limit_bytes=8 * 1024 * 1024),
    )(*(pltpu.with_memory_space_constraint(a, pltpu.HBM) for a in (features, solves.T, probes.T)))


def couple(features, scale, chunk, n_targets, n_sources, *refs):
    targets, sources, outs = refs[:n_targets], refs[n_targets : n_targets + n_sources], refs[n_targets + n_sources :]
    target = jnp.concatenate([ref[...] for ref in targets], axis=0)
    xt, wt = target[:, :features], target[:, features:]
    xt_pieces, wt_pieces = pieces(xt, 3), pieces(wt, 2)
    square_t = jnp.sum(xt * xt, axis=1, keepdims=True)
    ones = jnp.ones((8, features), jnp.bfloat16)
    totals, mixed = [], []
    for first in range(0, n_sources, chunk):
        source = jnp.concatenate([ref[...] for ref in sources[first : first + chunk]], axis=0)
        xs, ws = source[:, :features], source[:, features:]
        half = ws.shape[1] // 2
        ws = jnp.concatenate([ws[:, half:], ws[:, :half]], axis=1)
        xs_pieces = pieces(xs, 3)
        squares = [lax.dot_general(ones, part, NT, preferred_element_type=jnp.float32) for part in reversed(pieces(xs * xs, 3))]
        inner = product(xt_pieces, xs_pieces, NT)
        kernel = jnp.exp(inner - (0.5 * square_t + 0.5 * sum(squares)[:1]))
        coupling = kernel * product(wt_pieces, pieces(ws, 2), NT)
        totals.append(jnp.sum(coupling, axis=1, keepdims=True))
        mixed.append(product(pieces(coupling, 2), xs_pieces[:2], NN))
    value = scale * (xt * sum(totals) - sum(mixed))
    rows = outs[0].shape[0]
    for i, out in enumerate(outs):
        out[...] = value[i * rows : (i + 1) * rows]


def partial(features, scale, rows, targets, sources):
    n_t, n_s = (sum(block.shape[0] for block in blocks) for blocks in (targets, sources))
    chunk = min(4, len(sources))
    return pl.pallas_call(
        functools.partial(couple, features, scale, chunk, len(targets), len(sources)),
        out_shape=[jax.ShapeDtypeStruct((rows, features), jnp.float32) for _ in range(n_t // rows)],
        in_specs=[pl.BlockSpec(memory_space=pltpu.VMEM)] * (len(targets) + len(sources)),
        out_specs=[pl.BlockSpec(memory_space=pltpu.VMEM)] * (n_t // rows),
        cost_estimate=pl.CostEstimate(
            flops=24 * n_t * n_s * features, bytes_accessed=8 * (n_t + n_s) * features, transcendentals=n_t * n_s
        ),
        compiler_params=pltpu.CompilerParams(vmem_limit_bytes=32 * 1024 * 1024),
    )(*targets, *sources)


def local(total, features, solves, probes):
    width, vectors = features.shape[1], solves.shape[1]
    scale = -2.0 / (float(total) * float(vectors)) ** 0.5
    n_far, n_x, n_y = lax.axis_size("far"), lax.axis_size("x"), lax.axis_size("y")
    n_core = lax.axis_size("core")
    own = packed(features, solves, probes)

    def across(block):
        return [block] + [send(block, ("core",), (step,)) for step in range(1, n_core)]

    near = across(own)
    places = list(itertools.product(range(n_y), range(n_x)))
    far = [send(own, ("far",), (step,)) for step in range(n_far - 1, 0, -1)]
    gate = own
    beside = [own] + [send(gate, ("x",), (step,)) for step in range(1, n_x)]
    pair = jnp.concatenate(beside, axis=0)
    targets = beside + [send(pair, ("y",), (step,)) for step in range(1, n_y)]
    sources = near + [part for block in far for part in across(block)]
    sums = partial(width, scale, own.shape[0], targets, sources)

    out = sums[0]
    for place, part in zip(places[1:], sums[1:], strict=True):
        out = out + send(part, ("y", "x"), place, back=True)
    return out


def solution(mesh):
    n_row, n_col = mesh.shape["row"], mesh.shape["col"]
    n_core, n_x = (2 if n % 2 == 0 else 1 for n in (n_row, n_col))
    shape = (n_row // n_core, n_core, n_col // n_x, n_x)
    fine = Mesh(mesh.devices.reshape(shape), ("y", "core", "far", "x"))
    spec = P(("y", "core", "far", "x"), None)

    def run(features, solves, probes):
        inner = functools.partial(local, features.shape[0])
        return jax.shard_map(inner, mesh=fine, in_specs=(spec,) * 3, out_specs=spec, check_vma=False)(features, solves, probes)

    return run
```

time: 35.2 us -> 26.6 us (0.76)
  waiting for transfers between devices: 16.4 us -> 9.72 us
  local copies, waits for them, and re-layouts: 1.66 us -> 0 us
  Pallas kernels: 4.62 us -> 2.97 us
  starting transfers between devices: 11.4 us -> 13 us
    ppermute x11 -> x12, waiting for transfers between devices: 16.4 us -> 9.72 us  [send(): lax.ppermute(block, axes, [(j, i) for i, j in pairs] if back else pairs)]
    pallas_call x4 -> x2, Pallas kernels: 4.62 us -> 2.97 us  [the longest x1 2.08 us: partial(): pl.pallas_call(functools.partial(couple, features, scale, chunk, len(targ...]
    unnamed x6 -> x0, local copies, waits for them, and re-layouts: 1.64 us -> none
    ppermute x11 -> x12, starting transfers between devices: 11.4 us -> 13 us  [send(): lax.ppermute(block, axes, [(j, i) for i, j in pairs] if back else pairs)]
  transfers between devices with their start and end apart: 11 -> 12, of which waited for: 6 -> 6; matrix products, arithmetic and copies ran while one was open for 0% -> 0% of each run, Pallas kernels for 10% -> 0%
where the time goes in v2:
time: 26.6 us; the launch traced here: 26.4 us
  starting transfers between devices  13 us (49%)
  waiting for transfers between devices  9.72 us (37%)
  Pallas kernels  2.97 us (11%)
  other arithmetic  0.65 us (2%)
    ppermute x12, starting transfers between devices, send(): lax.ppermute(block, axes, [(j, i) for i, j in pairs] if back else pairs)  13 us
    ppermute x12, waiting for transfers between devices, send(): lax.ppermute(block, axes, [(j, i) for i, j in pairs] if back else pairs)  9.72 us
    pallas_call x1, Pallas kernels, partial(): pl.pallas_call(functools.partial(couple, features, scale, chunk, len(targ...  2.08 us
    pallas_call x1, Pallas kernels, packed(): pl.pallas_call(pack, out_shape=pltpu.VMEM((rows, width), jnp.float32), in...  0.89 us
    add x1, other arithmetic, local(): out = out + send(part, ('y', 'x'), place, back=True)  0.64 us
  transfers between devices with their start and end apart: 12, of which 6 were waited for; matrix products, arithmetic and copies ran while one was open for 0% of the time, Pallas kernels for 0%

profile of v2, /device:TPU:0, one launch (start us, length us, event | category | flops | bytes accessed | tf_op | source)
XLA Modules:
  0.0 26.4 jit_solution(3241862219611896683)
XLA Ops:
  0.0 0.9 %shard_map.37.refs_0_.refs_3_ = f32[96,256]{1,0:T(8,128)S(1)} custom-call(f32[96,128]{1,0:T(8,128)} %features_ref.1, f32[64,96]{1,0:T(8,128)} %bitcast.2, f32[64,96]{1,0:T(8,128)} %bitcast.3), custom_call_target="tpu_custom_call" | custom-call | tf_op jit(solution)/shard_map/pallas_call | solution.py:59
  0.9 3.0 %collective-permute-start = (f32[96,256]{1,0:T(8,128)S(1)}, f32[96,256]{1,0:T(8,128)S(1)}, u32[]{:S(2)}, u32[]{:S(2)}) collective-permute-start(f32[96,256]{1,0:T(8,128)S(1)} %shard_map.37.refs_0_.refs_3_), channel_id=1, source_target_pairs={{0,1},{1,0},{2,3},{3,2},{4,5},{5,4},{6,7},{7,6},{8,9},{9,8},{10,11... | collective-permute-start | bytes 294920 | tf_op jit(solution)/shard_map/ppermute | solution.py:24
  3.9 3.6 %collective-permute-start.3 = (f32[96,256]{1,0:T(8,128)S(1)}, f32[96,256]{1,0:T(8,128)S(1)}, u32[]{:S(2)}, u32[]{:S(2)}) collective-permute-start(f32[96,256]{1,0:T(8,128)S(1)} %shard_map.37.refs_0_.refs_3_), channel_id=1, source_target_pairs={{0,6},{2,4},{4,2},{6,0},{1,7},{3,5},{5,3},{7,1},{8,14},{10,12},{12... | collective-permute-start | bytes 294920 | tf_op jit(solution)/shard_map/ppermute | solution.py:24
  7.5 0.0 collective-permute-start.5
  7.5 0.8 %collective-permute-start.7 = (f32[96,256]{1,0:T(8,128)S(1)}, f32[96,256]{1,0:T(8,128)S(1)}, u32[]{:S(2)}, u32[]{:S(2)}) collective-permute-start(f32[96,256]{1,0:T(8,128)S(1)} %shard_map.37.refs_0_.refs_3_), channel_id=1, source_target_pairs={{0,2},{2,0},{4,6},{6,4},{1,3},{3,1},{5,7},{7,5},{8,10},{10,8},{12,... | collective-permute-start | bytes 294920 | tf_op jit(solution)/shard_map/ppermute | solution.py:24
  8.3 0.0 collective-permute-done.refs_1_
  8.3 1.6 %collective-permute-start.1 = (f32[192,256]{1,0:T(8,128)S(1)}, f32[192,256]{1,0:T(8,128)S(1)}, u32[]{:S(2)}, u32[]{:S(2)}) collective-permute-start(f32[192,256]{1,0:T(8,128)S(1)} %pad_maximum_fusion), channel_id=1, source_target_pairs={{0,16},{16,0},{1,17},{17,1},{2,18},{18,2},{3,19},{19,3},{4,20},{20... | collective-permute-start | bytes 589832 | tf_op jit(solution)/shard_map/ppermute | solution.py:24
  9.9 0.0 collective-permute-start.2
  9.9 1.5 %collective-permute-done.3.refs_5_ = f32[96,256]{1,0:T(8,128)S(1)} collective-permute-done((f32[96,256]{1,0:T(8,128)S(1)}, f32[96,256]{1,0:T(8,128)S(1)}, u32[]{:S(2)}, u32[]{:S(2)}) %collective-permute-start.3) | collective-permute-done | bytes 98336 | tf_op jit(solution)/shard_map/ppermute | solution.py:24
  11.4 0.0 collective-permute-start.4
  11.4 4.1 %collective-permute-done.5.refs_7_ = f32[96,256]{1,0:T(8,128)S(1)} collective-permute-done((f32[96,256]{1,0:T(8,128)S(1)}, f32[96,256]{1,0:T(8,128)S(1)}, u32[]{:S(2)}, u32[]{:S(2)}) %collective-permute-start.5) | collective-permute-done | bytes 98336 | tf_op jit(solution)/shard_map/ppermute | solution.py:24
  15.5 0.0 collective-permute-start.6
  15.5 0.0 collective-permute-done.7.refs_9_
  15.5 0.5 %collective-permute-start.8 = (f32[96,256]{1,0:T(8,128)S(1)}, f32[96,256]{1,0:T(8,128)S(1)}, u32[]{:S(2)}, u32[]{:S(2)}) collective-permute-start(f32[96,256]{1,0:T(8,128)S(1)} %collective-permute-done.7.refs_9_), channel_id=1, source_target_pairs={{0,8},{8,0},{1,9},{9,1},{2,10},{10,2},{3,11},{11,3},{4,12},{12,4},... | collective-permute-start | bytes 294920 | tf_op jit(solution)/shard_map/ppermute | solution.py:24
  16.0 0.0 collective-permute-done.2.refs_4_
  16.0 0.0 collective-permute-done.4.refs_6_
  16.0 0.8 %collective-permute-done.6.refs_8_ = f32[96,256]{1,0:T(8,128)S(1)} collective-permute-done((f32[96,256]{1,0:T(8,128)S(1)}, f32[96,256]{1,0:T(8,128)S(1)}, u32[]{:S(2)}, u32[]{:S(2)}) %collective-permute-start.6) | collective-permute-done | bytes 98336 | tf_op jit(solution)/shard_map/ppermute | solution.py:24
  16.8 0.2 collective-permute-done.8.refs_10_
  17.0 0.0 collective-permute-done.1.refs_2_
  17.0 2.1 %shard_map.38 = (f32[96,128]{1,0:T(8,128)S(1)}, f32[96,128]{1,0:T(8,128)S(1)}, f32[96,128]{1,0:T(8,128)S(1)}, f32[96,128]{1,0:T(8,128)S(1)}) custom-call(f32[96,256]{1,0:T(8,128)S(1)} %shard_map.37.refs_0_.refs_3_, f32[96,256]{1,0:T(8,128)S(1)} %collective-permute-done.refs_1_, f32[192,256]{1,0:T(8,128)S(1)} %collective-permute-done.1.refs_2_, ...), custom_call_target="tpu_custom_call" | custom-call | flops 905969664 | bytes 1179648 | tf_op jit(solution)/shard_map/pallas_call | solution.py:101
  19.0 1.6 %collective-permute-start.10 = (f32[96,128]{1,0:T(8,128)S(1)}, f32[96,128]{1,0:T(8,128)S(1)}, u32[]{:S(2)}, u32[]{:S(2)}) collective-permute-start(f32[96,128]{1,0:T(8,128)S(1)} %get-tuple-element.11), channel_id=1, source_target_pairs={{16,0},{17,1},{0,16},{1,17},{18,2},{19,3},{2,18},{3,19},{20,4},{21... | collective-permute-start | bytes 147464 | tf_op jit(solution)/shard_map/ppermute | solution.py:24
  20.6 0.5 %collective-permute-start.11 = (f32[96,128]{1,0:T(8,128)S(1)}, f32[96,128]{1,0:T(8,128)S(1)}, u32[]{:S(2)}, u32[]{:S(2)}) collective-permute-start(f32[96,128]{1,0:T(8,128)S(1)} %get-tuple-element.12), channel_id=1, source_target_pairs={{17,0},{16,1},{1,16},{0,17},{19,2},{18,3},{3,18},{2,19},{21,4},{20... | collective-permute-start | bytes 147464 | tf_op jit(solution)/shard_map/ppermute | solution.py:24
  21.1 1.5 %collective-permute-start.9 = (f32[96,128]{1,0:T(8,128)S(1)}, f32[96,128]{1,0:T(8,128)S(1)}, u32[]{:S(2)}, u32[]{:S(2)}) collective-permute-start(f32[96,128]{1,0:T(8,128)S(1)} %get-tuple-element.10), channel_id=1, source_target_pairs={{1,0},{0,1},{17,16},{16,17},{3,2},{2,3},{19,18},{18,19},{5,4},{4,5... | collective-permute-start | bytes 147464 | tf_op jit(solution)/shard_map/ppermute | solution.py:24
  22.6 0.6 %collective-permute-done.10 = f32[96,128]{1,0:T(8,128)S(1)} collective-permute-done((f32[96,128]{1,0:T(8,128)S(1)}, f32[96,128]{1,0:T(8,128)S(1)}, u32[]{:S(2)}, u32[]{:S(2)}) %collective-permute-start.10) | collective-permute-done | bytes 49184 | tf_op jit(solution)/shard_map/ppermute | solution.py:24
  23.2 2.6 %collective-permute-done.11 = f32[96,128]{1,0:T(8,128)S(1)} collective-permute-done((f32[96,128]{1,0:T(8,128)S(1)}, f32[96,128]{1,0:T(8,128)S(1)}, u32[]{:S(2)}, u32[]{:S(2)}) %collective-permute-start.11) | collective-permute-done | bytes 49184 | tf_op jit(solution)/shard_map/ppermute | solution.py:24
  25.8 0.0 collective-permute-done.9
  25.8 0.6 %add_add_fusion = f32[96,128]{1,0:T(8,128)} fusion(f32[96,128]{1,0:T(8,128)S(1)} %collective-permute-done.11, f32[96,128]{1,0:T(8,128)S(1)} %collective-permute-done.10, f32[96,128]{1,0:T(8,128)S(1)} %get-tuple-element.9, f32[96,128]{1,0:T(8,128)S(1)} %collective-permute-done.9), kind=kLoop, calls=%fused_computation.1 | loop fusion | flops 36864 | bytes 245760 | tf_op jit(solution)/shard_map/add | solution.py:135
  (1 shorter events, 0.0 us)
Async XLA Ops:
  0.9 7.4 %collective-permute-start = (f32[96,256]{1,0:T(8,128)S(1)}, f32[96,256]{1,0:T(8,128)S(1)}, u32[]{:S(2)}, u32[]{:S(2)}) collective-permute-start(f32[96,256]{1,0:T(8,128)S(1)} %shard_map.37.refs_0_.refs_3_), channel_id=1, source_target_pairs={{0,1},{1,0},{2,3},{3,2},{4,5},{5,4},{6,7},{7,6},{8,9},{9,8},{10,11... | collective-permute-start | bytes 294920 | tf_op jit(solution)/shard_map/ppermute | solution.py:24
  3.9 7.5 %collective-permute-start.3 = (f32[96,256]{1,0:T(8,128)S(1)}, f32[96,256]{1,0:T(8,128)S(1)}, u32[]{:S(2)}, u32[]{:S(2)}) collective-permute-start(f32[96,256]{1,0:T(8,128)S(1)} %shard_map.37.refs_0_.refs_3_), channel_id=1, source_target_pairs={{0,6},{2,4},{4,2},{6,0},{1,7},{3,5},{5,3},{7,1},{8,14},{10,12},{12... | collective-permute-start | bytes 294920 | tf_op jit(solution)/shard_map/ppermute | solution.py:24
  7.5 8.0 %collective-permute-start.5 = (f32[96,256]{1,0:T(8,128)S(1)}, f32[96,256]{1,0:T(8,128)S(1)}, u32[]{:S(2)}, u32[]{:S(2)}) collective-permute-start(f32[96,256]{1,0:T(8,128)S(1)} %shard_map.37.refs_0_.refs_3_), channel_id=1, source_target_pairs={{0,4},{2,6},{4,0},{6,2},{1,5},{3,7},{5,1},{7,3},{8,12},{10,14},{12... | collective-permute-start | bytes 294920 | tf_op jit(solution)/shard_map/ppermute | solution.py:24
  7.5 8.0 %collective-permute-start.7 = (f32[96,256]{1,0:T(8,128)S(1)}, f32[96,256]{1,0:T(8,128)S(1)}, u32[]{:S(2)}, u32[]{:S(2)}) collective-permute-start(f32[96,256]{1,0:T(8,128)S(1)} %shard_map.37.refs_0_.refs_3_), channel_id=1, source_target_pairs={{0,2},{2,0},{4,6},{6,4},{1,3},{3,1},{5,7},{7,5},{8,10},{10,8},{12,... | collective-permute-start | bytes 294920 | tf_op jit(solution)/shard_map/ppermute | solution.py:24
  8.3 8.6 %collective-permute-start.1 = (f32[192,256]{1,0:T(8,128)S(1)}, f32[192,256]{1,0:T(8,128)S(1)}, u32[]{:S(2)}, u32[]{:S(2)}) collective-permute-start(f32[192,256]{1,0:T(8,128)S(1)} %pad_maximum_fusion), channel_id=1, source_target_pairs={{0,16},{16,0},{1,17},{17,1},{2,18},{18,2},{3,19},{19,3},{4,20},{20... | collective-permute-start | bytes 589832 | tf_op jit(solution)/shard_map/ppermute | solution.py:24
  9.9 6.1 %collective-permute-start.2 = (f32[96,256]{1,0:T(8,128)S(1)}, f32[96,256]{1,0:T(8,128)S(1)}, u32[]{:S(2)}, u32[]{:S(2)}) collective-permute-start(f32[96,256]{1,0:T(8,128)S(1)} %shard_map.37.refs_0_.refs_3_), channel_id=1, source_target_pairs={{0,8},{8,0},{1,9},{9,1},{2,10},{10,2},{3,11},{11,3},{4,12},{12,4},... | collective-permute-start | bytes 294920 | tf_op jit(solution)/shard_map/ppermute | solution.py:24
  11.4 4.6 %collective-permute-start.4 = (f32[96,256]{1,0:T(8,128)S(1)}, f32[96,256]{1,0:T(8,128)S(1)}, u32[]{:S(2)}, u32[]{:S(2)}) collective-permute-start(f32[96,256]{1,0:T(8,128)S(1)} %collective-permute-done.3.refs_5_), channel_id=1, source_target_pairs={{0,8},{8,0},{1,9},{9,1},{2,10},{10,2},{3,11},{11,3},{4,12},{12,4},... | collective-permute-start | bytes 294920 | tf_op jit(solution)/shard_map/ppermute | solution.py:24
  15.5 1.3 %collective-permute-start.6 = (f32[96,256]{1,0:T(8,128)S(1)}, f32[96,256]{1,0:T(8,128)S(1)}, u32[]{:S(2)}, u32[]{:S(2)}) collective-permute-start(f32[96,256]{1,0:T(8,128)S(1)} %collective-permute-done.5.refs_7_), channel_id=1, source_target_pairs={{0,8},{8,0},{1,9},{9,1},{2,10},{10,2},{3,11},{11,3},{4,12},{12,4},... | collective-permute-start | bytes 294920 | tf_op jit(solution)/shard_map/ppermute | solution.py:24
  15.5 1.5 %collective-permute-start.8 = (f32[96,256]{1,0:T(8,128)S(1)}, f32[96,256]{1,0:T(8,128)S(1)}, u32[]{:S(2)}, u32[]{:S(2)}) collective-permute-start(f32[96,256]{1,0:T(8,128)S(1)} %collective-permute-done.7.refs_9_), channel_id=1, source_target_pairs={{0,8},{8,0},{1,9},{9,1},{2,10},{10,2},{3,11},{11,3},{4,12},{12,4},... | collective-permute-start | bytes 294920 | tf_op jit(solution)/shard_map/ppermute | solution.py:24
  19.0 4.2 %collective-permute-start.10 = (f32[96,128]{1,0:T(8,128)S(1)}, f32[96,128]{1,0:T(8,128)S(1)}, u32[]{:S(2)}, u32[]{:S(2)}) collective-permute-start(f32[96,128]{1,0:T(8,128)S(1)} %get-tuple-element.11), channel_id=1, source_target_pairs={{16,0},{17,1},{0,16},{1,17},{18,2},{19,3},{2,18},{3,19},{20,4},{21... | collective-permute-start | bytes 147464 | tf_op jit(solution)/shard_map/ppermute | solution.py:24
  20.6 5.1 %collective-permute-start.11 = (f32[96,128]{1,0:T(8,128)S(1)}, f32[96,128]{1,0:T(8,128)S(1)}, u32[]{:S(2)}, u32[]{:S(2)}) collective-permute-start(f32[96,128]{1,0:T(8,128)S(1)} %get-tuple-element.12), channel_id=1, source_target_pairs={{17,0},{16,1},{1,16},{0,17},{19,2},{18,3},{3,18},{2,19},{21,4},{20... | collective-permute-start | bytes 147464 | tf_op jit(solution)/shard_map/ppermute | solution.py:24
  21.1 4.7 %collective-permute-start.9 = (f32[96,128]{1,0:T(8,128)S(1)}, f32[96,128]{1,0:T(8,128)S(1)}, u32[]{:S(2)}, u32[]{:S(2)}) collective-permute-start(f32[96,128]{1,0:T(8,128)S(1)} %get-tuple-element.10), channel_id=1, source_target_pairs={{1,0},{0,1},{17,16},{16,17},{3,2},{2,3},{19,18},{18,19},{5,4},{4,5... | collective-permute-start | bytes 147464 | tf_op jit(solution)/shard_map/ppermute | solution.py:24

commit v3 on v2

--- a/solution.py
+++ b/solution.py
@@ -69,45 +69,46 @@
     )(*(pltpu.with_memory_space_constraint(a, pltpu.HBM) for a in (features, solves.T, probes.T)))
 
 
-def couple(features, scale, chunk, n_targets, n_sources, *refs):
-    targets, sources, outs = refs[:n_targets], refs[n_targets : n_targets + n_sources], refs[n_targets + n_sources :]
+def couple(features, scale, counts, *refs):
+    targets, sources, sums, outs = (refs[sum(counts[:i]) : sum(counts[: i + 1])] for i in range(4))
     target = jnp.concatenate([ref[...] for ref in targets], axis=0)
+    source = jnp.concatenate([ref[...] for ref in sources], axis=0)
     xt, wt = target[:, :features], target[:, features:]
-    xt_pieces, wt_pieces = pieces(xt, 3), pieces(wt, 2)
+    xs, ws = source[:, :features], source[:, features:]
+    half = ws.shape[1] // 2
+    ws = jnp.concatenate([ws[:, half:], ws[:, :half]], axis=1)
+    xs_pieces = pieces(xs, 3)
     square_t = jnp.sum(xt * xt, axis=1, keepdims=True)
     ones = jnp.ones((8, features), jnp.bfloat16)
-    totals, mixed = [], []
-    for first in range(0, n_sources, chunk):
-        source = jnp.concatenate([ref[...] for ref in sources[first : first + chunk]], axis=0)
-        xs, ws = source[:, :features], source[:, features:]
-        half = ws.shape[1] // 2
-        ws = jnp.concatenate([ws[:, half:], ws[:, :half]], axis=1)
-        xs_pieces = pieces(xs, 3)
-        squares = [lax.dot_general(ones, part, NT, preferred_element_type=jnp.float32) for part in reversed(pieces(xs * xs, 3))]
-        inner = product(xt_pieces, xs_pieces, NT)
-        kernel = jnp.exp(inner - (0.5 * square_t + 0.5 * sum(squares)[:1]))
-        coupling = kernel * product(wt_pieces, pieces(ws, 2), NT)
-        totals.append(jnp.sum(coupling, axis=1, keepdims=True))
-        mixed.append(product(pieces(coupling, 2), xs_pieces[:2], NN))
-    value = scale * (xt * sum(totals) - sum(mixed))
+    squares = [lax.dot_general(ones, part, NT, preferred_element_type=jnp.float32) for part in reversed(pieces(xs * xs, 3))]
+    inner = product(pieces(xt, 3), xs_pieces, NT)
+    kernel = jnp.exp(inner - (0.5 * square_t + 0.5 * sum(squares)[:1]))
+    coupling = kernel * product(pieces(wt, 2), pieces(ws, 2), NT)
+    totals = jnp.sum(coupling, axis=1, keepdims=True)
+    upper, lower = xs_pieces[:2]
+    right = jnp.concatenate(
+        [jnp.concatenate([upper, lower], axis=1), jnp.concatenate([upper, jnp.zeros_like(lower)], axis=1)], axis=0
+    )
+    both = lax.dot_general(jnp.concatenate(pieces(coupling, 2), axis=1), right, NN, preferred_element_type=jnp.float32)
+    value = scale * (xt * totals - (both[:, :features] + both[:, features:]))
     rows = outs[0].shape[0]
     for i, out in enumerate(outs):
-        out[...] = value[i * rows : (i + 1) * rows]
+        part = value[i * rows : (i + 1) * rows]
+        out[...] = part + sums[i][...] if sums else part
 
 
-def partial(features, scale, rows, targets, sources):
+def partial(features, scale, rows, targets, sources, sums=()):
     n_t, n_s = (sum(block.shape[0] for block in blocks) for blocks in (targets, sources))
-    chunk = min(4, len(sources))
     return pl.pallas_call(
-        functools.partial(couple, features, scale, chunk, len(targets), len(sources)),
+        functools.partial(couple, features, scale, (len(targets), len(sources), len(sums), n_t // rows)),
         out_shape=[jax.ShapeDtypeStruct((rows, features), jnp.float32) for _ in range(n_t // rows)],
-        in_specs=[pl.BlockSpec(memory_space=pltpu.VMEM)] * (len(targets) + len(sources)),
+        in_specs=[pl.BlockSpec(memory_space=pltpu.VMEM)] * (len(targets) + len(sources) + len(sums)),
         out_specs=[pl.BlockSpec(memory_space=pltpu.VMEM)] * (n_t // rows),
         cost_estimate=pl.CostEstimate(
             flops=24 * n_t * n_s * features, bytes_accessed=8 * (n_t + n_s) * features, transcendentals=n_t * n_s
         ),
         compiler_params=pltpu.CompilerParams(vmem_limit_bytes=32 * 1024 * 1024),
-    )(*targets, *sources)
+    )(*targets, *sources, *sums)
 
 
 def local(total, features, solves, probes):
@@ -122,17 +123,18 @@
 
     near = across(own)
     places = list(itertools.product(range(n_y), range(n_x)))
-    far = [send(own, ("far",), (step,)) for step in range(n_far - 1, 0, -1)]
+    far = [send(own, ("far",), (step,)) for step in sorted(range(1, n_far), key=lambda step: (step != n_far // 2, step))]
     gate = own
     beside = [own] + [send(gate, ("x",), (step,)) for step in range(1, n_x)]
     pair = jnp.concatenate(beside, axis=0)
     targets = beside + [send(pair, ("y",), (step,)) for step in range(1, n_y)]
     sources = near + [part for block in far for part in across(block)]
     sums = partial(width, scale, own.shape[0], targets, sources)
-
+    order = sorted(range(1, len(places)), key=lambda i: places[i][1] == 0)
+    returned = [send(sums[i], ("y", "x"), places[i], back=True) for i in order]
     out = sums[0]
-    for place, part in zip(places[1:], sums[1:], strict=True):
-        out = out + send(part, ("y", "x"), place, back=True)
+    for part in returned:
+        out = out + part
     return out
 
 

time: 26.6 us -> 24.6 us (0.925)
  waiting for transfers between devices: 9.72 us -> 8.01 us
    ppermute x12, waiting for transfers between devices: 9.72 us -> 8.01 us  [send(): lax.ppermute(block, axes, [(j, i) for i, j in pairs] if back else pairs)]
where the time goes in v3:
time: 24.6 us; the launch traced here: 24.5 us
  starting transfers between devices  13 us (53%)
  waiting for transfers between devices  8.01 us (33%)
  Pallas kernels  2.72 us (11%)
  other arithmetic  0.65 us (3%)
    ppermute x12, starting transfers between devices, send(): lax.ppermute(block, axes, [(j, i) for i, j in pairs] if back else pairs)  13 us
    ppermute x12, waiting for transfers between devices, send(): lax.ppermute(block, axes, [(j, i) for i, j in pairs] if back else pairs)  8.01 us
    pallas_call x1, Pallas kernels, partial(): pl.pallas_call(functools.partial(couple, features, scale, (len(targets),...  1.83 us
    pallas_call x1, Pallas kernels, packed(): pl.pallas_call(pack, out_shape=pltpu.VMEM((rows, width), jnp.float32), in...  0.89 us
    add x1, other arithmetic, local(): out = out + part  0.64 us
  transfers between devices with their start and end apart: 12, of which 6 were waited for; matrix products, arithmetic and copies ran while one was open for 0% of the time, Pallas kernels for 0%

profile of v3, /device:TPU:0, one launch (start us, length us, event | category | flops | bytes accessed | tf_op | source)
XLA Modules:
  0.0 24.5 jit_solution(2664151158454827424)
XLA Ops:
  0.0 0.9 %shard_map.37.refs_0_.refs_3_ = f32[96,256]{1,0:T(8,128)S(1)} custom-call(f32[96,128]{1,0:T(8,128)} %features_ref.1, f32[64,96]{1,0:T(8,128)} %bitcast.2, f32[64,96]{1,0:T(8,128)} %bitcast.3), custom_call_target="tpu_custom_call" | custom-call | tf_op jit(solution)/shard_map/pallas_call | solution.py:59
  0.9 3.0 %collective-permute-start = (f32[96,256]{1,0:T(8,128)S(1)}, f32[96,256]{1,0:T(8,128)S(1)}, u32[]{:S(2)}, u32[]{:S(2)}) collective-permute-start(f32[96,256]{1,0:T(8,128)S(1)} %shard_map.37.refs_0_.refs_3_), channel_id=1, source_target_pairs={{0,1},{1,0},{2,3},{3,2},{4,5},{5,4},{6,7},{7,6},{8,9},{9,8},{10,11... | collective-permute-start | bytes 294920 | tf_op jit(solution)/shard_map/ppermute | solution.py:24
  3.9 2.6 %collective-permute-start.3 = (f32[96,256]{1,0:T(8,128)S(1)}, f32[96,256]{1,0:T(8,128)S(1)}, u32[]{:S(2)}, u32[]{:S(2)}) collective-permute-start(f32[96,256]{1,0:T(8,128)S(1)} %shard_map.37.refs_0_.refs_3_), channel_id=1, source_target_pairs={{0,4},{2,6},{4,0},{6,2},{1,5},{3,7},{5,1},{7,3},{8,12},{10,14},{12... | collective-permute-start | bytes 294920 | tf_op jit(solution)/shard_map/ppermute | solution.py:24
  6.5 1.6 %collective-permute-start.5 = (f32[96,256]{1,0:T(8,128)S(1)}, f32[96,256]{1,0:T(8,128)S(1)}, u32[]{:S(2)}, u32[]{:S(2)}) collective-permute-start(f32[96,256]{1,0:T(8,128)S(1)} %shard_map.37.refs_0_.refs_3_), channel_id=1, source_target_pairs={{0,2},{2,0},{4,6},{6,4},{1,3},{3,1},{5,7},{7,5},{8,10},{10,8},{12,... | collective-permute-start | bytes 294920 | tf_op jit(solution)/shard_map/ppermute | solution.py:24
  8.1 0.2 collective-permute-start.7
  8.3 0.0 collective-permute-done.refs_1_
  8.3 1.6 %collective-permute-start.1 = (f32[192,256]{1,0:T(8,128)S(1)}, f32[192,256]{1,0:T(8,128)S(1)}, u32[]{:S(2)}, u32[]{:S(2)}) collective-permute-start(f32[192,256]{1,0:T(8,128)S(1)} %pad_maximum_fusion), channel_id=1, source_target_pairs={{0,16},{16,0},{1,17},{17,1},{2,18},{18,2},{3,19},{19,3},{4,20},{20... | collective-permute-start | bytes 589832 | tf_op jit(solution)/shard_map/ppermute | solution.py:24
  9.9 0.0 collective-permute-start.2
  9.9 2.1 %collective-permute-done.3.refs_5_ = f32[96,256]{1,0:T(8,128)S(1)} collective-permute-done((f32[96,256]{1,0:T(8,128)S(1)}, f32[96,256]{1,0:T(8,128)S(1)}, u32[]{:S(2)}, u32[]{:S(2)}) %collective-permute-start.3) | collective-permute-done | bytes 98336 | tf_op jit(solution)/shard_map/ppermute | solution.py:24
  12.0 0.0 collective-permute-start.4
  12.0 0.0 collective-permute-done.5.refs_7_
  12.0 0.5 %collective-permute-start.6 = (f32[96,256]{1,0:T(8,128)S(1)}, f32[96,256]{1,0:T(8,128)S(1)}, u32[]{:S(2)}, u32[]{:S(2)}) collective-permute-start(f32[96,256]{1,0:T(8,128)S(1)} %collective-permute-done.5.refs_7_), channel_id=1, source_target_pairs={{0,8},{8,0},{1,9},{9,1},{2,10},{10,2},{3,11},{11,3},{4,12},{12,4},... | collective-permute-start | bytes 294920 | tf_op jit(solution)/shard_map/ppermute | solution.py:24
  12.5 2.0 %collective-permute-done.7.refs_9_ = f32[96,256]{1,0:T(8,128)S(1)} collective-permute-done((f32[96,256]{1,0:T(8,128)S(1)}, f32[96,256]{1,0:T(8,128)S(1)}, u32[]{:S(2)}, u32[]{:S(2)}) %collective-permute-start.7) | collective-permute-done | bytes 98336 | tf_op jit(solution)/shard_map/ppermute | solution.py:24
  14.5 0.0 collective-permute-start.8
  14.5 0.0 collective-permute-done.2.refs_4_
  14.6 0.0 collective-permute-done.4.refs_6_
  14.6 0.0 collective-permute-done.6.refs_8_
  14.6 1.3 %collective-permute-done.8.refs_10_ = f32[96,256]{1,0:T(8,128)S(1)} collective-permute-done((f32[96,256]{1,0:T(8,128)S(1)}, f32[96,256]{1,0:T(8,128)S(1)}, u32[]{:S(2)}, u32[]{:S(2)}) %collective-permute-start.8) | collective-permute-done | bytes 98336 | tf_op jit(solution)/shard_map/ppermute | solution.py:24
  15.8 0.0 collective-permute-done.1.refs_2_
  15.8 1.8 %shard_map.38 = (f32[96,128]{1,0:T(8,128)S(1)}, f32[96,128]{1,0:T(8,128)S(1)}, f32[96,128]{1,0:T(8,128)S(1)}, f32[96,128]{1,0:T(8,128)S(1)}) custom-call(f32[96,256]{1,0:T(8,128)S(1)} %shard_map.37.refs_0_.refs_3_, f32[96,256]{1,0:T(8,128)S(1)} %collective-permute-done.refs_1_, f32[192,256]{1,0:T(8,128)S(1)} %collective-permute-done.1.refs_2_, ...), custom_call_target="tpu_custom_call" | custom-call | flops 905969664 | bytes 1179648 | tf_op jit(solution)/shard_map/pallas_call | solution.py:102
  17.7 1.6 %collective-permute-start.10 = (f32[96,128]{1,0:T(8,128)S(1)}, f32[96,128]{1,0:T(8,128)S(1)}, u32[]{:S(2)}, u32[]{:S(2)}) collective-permute-start(f32[96,128]{1,0:T(8,128)S(1)} %get-tuple-element.11), channel_id=1, source_target_pairs={{17,0},{16,1},{1,16},{0,17},{19,2},{18,3},{3,18},{2,19},{21,4},{20... | collective-permute-start | bytes 147464 | tf_op jit(solution)/shard_map/ppermute | solution.py:24
  19.2 0.5 %collective-permute-start.11 = (f32[96,128]{1,0:T(8,128)S(1)}, f32[96,128]{1,0:T(8,128)S(1)}, u32[]{:S(2)}, u32[]{:S(2)}) collective-permute-start(f32[96,128]{1,0:T(8,128)S(1)} %get-tuple-element.12), channel_id=1, source_target_pairs={{16,0},{17,1},{0,16},{1,17},{18,2},{19,3},{2,18},{3,19},{20,4},{21... | collective-permute-start | bytes 147464 | tf_op jit(solution)/shard_map/ppermute | solution.py:24
  19.7 1.5 %collective-permute-start.9 = (f32[96,128]{1,0:T(8,128)S(1)}, f32[96,128]{1,0:T(8,128)S(1)}, u32[]{:S(2)}, u32[]{:S(2)}) collective-permute-start(f32[96,128]{1,0:T(8,128)S(1)} %get-tuple-element.10), channel_id=1, source_target_pairs={{1,0},{0,1},{17,16},{16,17},{3,2},{2,3},{19,18},{18,19},{5,4},{4,5... | collective-permute-start | bytes 147464 | tf_op jit(solution)/shard_map/ppermute | solution.py:24
  21.2 1.6 %collective-permute-done.10 = f32[96,128]{1,0:T(8,128)S(1)} collective-permute-done((f32[96,128]{1,0:T(8,128)S(1)}, f32[96,128]{1,0:T(8,128)S(1)}, u32[]{:S(2)}, u32[]{:S(2)}) %collective-permute-start.10) | collective-permute-done | bytes 49184 | tf_op jit(solution)/shard_map/ppermute | solution.py:24
  22.8 0.7 %collective-permute-done.11 = f32[96,128]{1,0:T(8,128)S(1)} collective-permute-done((f32[96,128]{1,0:T(8,128)S(1)}, f32[96,128]{1,0:T(8,128)S(1)}, u32[]{:S(2)}, u32[]{:S(2)}) %collective-permute-start.11) | collective-permute-done | bytes 49184 | tf_op jit(solution)/shard_map/ppermute | solution.py:24
  23.5 0.3 %collective-permute-done.9 = f32[96,128]{1,0:T(8,128)S(1)} collective-permute-done((f32[96,128]{1,0:T(8,128)S(1)}, f32[96,128]{1,0:T(8,128)S(1)}, u32[]{:S(2)}, u32[]{:S(2)}) %collective-permute-start.9) | collective-permute-done | bytes 49184 | tf_op jit(solution)/shard_map/ppermute | solution.py:24
  23.8 0.6 %add_add_fusion = f32[96,128]{1,0:T(8,128)} fusion(f32[96,128]{1,0:T(8,128)S(1)} %collective-permute-done.11, f32[96,128]{1,0:T(8,128)S(1)} %collective-permute-done.10, f32[96,128]{1,0:T(8,128)S(1)} %get-tuple-element.9, f32[96,128]{1,0:T(8,128)S(1)} %collective-permute-done.9), kind=kLoop, calls=%fused_computation.1 | loop fusion | flops 36864 | bytes 245760 | tf_op jit(solution)/shard_map/add | solution.py:137
  (1 shorter events, 0.0 us)
Async XLA Ops:
  0.9 7.4 %collective-permute-start = (f32[96,256]{1,0:T(8,128)S(1)}, f32[96,256]{1,0:T(8,128)S(1)}, u32[]{:S(2)}, u32[]{:S(2)}) collective-permute-start(f32[96,256]{1,0:T(8,128)S(1)} %shard_map.37.refs_0_.refs_3_), channel_id=1, source_target_pairs={{0,1},{1,0},{2,3},{3,2},{4,5},{5,4},{6,7},{7,6},{8,9},{9,8},{10,11... | collective-permute-start | bytes 294920 | tf_op jit(solution)/shard_map/ppermute | solution.py:24
  3.9 8.1 %collective-permute-start.3 = (f32[96,256]{1,0:T(8,128)S(1)}, f32[96,256]{1,0:T(8,128)S(1)}, u32[]{:S(2)}, u32[]{:S(2)}) collective-permute-start(f32[96,256]{1,0:T(8,128)S(1)} %shard_map.37.refs_0_.refs_3_), channel_id=1, source_target_pairs={{0,4},{2,6},{4,0},{6,2},{1,5},{3,7},{5,1},{7,3},{8,12},{10,14},{12... | collective-permute-start | bytes 294920 | tf_op jit(solution)/shard_map/ppermute | solution.py:24
  6.5 5.5 %collective-permute-start.5 = (f32[96,256]{1,0:T(8,128)S(1)}, f32[96,256]{1,0:T(8,128)S(1)}, u32[]{:S(2)}, u32[]{:S(2)}) collective-permute-start(f32[96,256]{1,0:T(8,128)S(1)} %shard_map.37.refs_0_.refs_3_), channel_id=1, source_target_pairs={{0,2},{2,0},{4,6},{6,4},{1,3},{3,1},{5,7},{7,5},{8,10},{10,8},{12,... | collective-permute-start | bytes 294920 | tf_op jit(solution)/shard_map/ppermute | solution.py:24
  8.1 6.5 %collective-permute-start.7 = (f32[96,256]{1,0:T(8,128)S(1)}, f32[96,256]{1,0:T(8,128)S(1)}, u32[]{:S(2)}, u32[]{:S(2)}) collective-permute-start(f32[96,256]{1,0:T(8,128)S(1)} %shard_map.37.refs_0_.refs_3_), channel_id=1, source_target_pairs={{0,6},{2,4},{4,2},{6,0},{1,7},{3,5},{5,3},{7,1},{8,14},{10,12},{12... | collective-permute-start | bytes 294920 | tf_op jit(solution)/shard_map/ppermute | solution.py:24
  8.3 7.5 %collective-permute-start.1 = (f32[192,256]{1,0:T(8,128)S(1)}, f32[192,256]{1,0:T(8,128)S(1)}, u32[]{:S(2)}, u32[]{:S(2)}) collective-permute-start(f32[192,256]{1,0:T(8,128)S(1)} %pad_maximum_fusion), channel_id=1, source_target_pairs={{0,16},{16,0},{1,17},{17,1},{2,18},{18,2},{3,19},{19,3},{4,20},{20... | collective-permute-start | bytes 589832 | tf_op jit(solution)/shard_map/ppermute | solution.py:24
  9.9 4.7 %collective-permute-start.2 = (f32[96,256]{1,0:T(8,128)S(1)}, f32[96,256]{1,0:T(8,128)S(1)}, u32[]{:S(2)}, u32[]{:S(2)}) collective-permute-start(f32[96,256]{1,0:T(8,128)S(1)} %shard_map.37.refs_0_.refs_3_), channel_id=1, source_target_pairs={{0,8},{8,0},{1,9},{9,1},{2,10},{10,2},{3,11},{11,3},{4,12},{12,4},... | collective-permute-start | bytes 294920 | tf_op jit(solution)/shard_map/ppermute | solution.py:24
  12.0 2.6 %collective-permute-start.4 = (f32[96,256]{1,0:T(8,128)S(1)}, f32[96,256]{1,0:T(8,128)S(1)}, u32[]{:S(2)}, u32[]{:S(2)}) collective-permute-start(f32[96,256]{1,0:T(8,128)S(1)} %collective-permute-done.3.refs_5_), channel_id=1, source_target_pairs={{0,8},{8,0},{1,9},{9,1},{2,10},{10,2},{3,11},{11,3},{4,12},{12,4},... | collective-permute-start | bytes 294920 | tf_op jit(solution)/shard_map/ppermute | solution.py:24
  12.0 2.6 %collective-permute-start.6 = (f32[96,256]{1,0:T(8,128)S(1)}, f32[96,256]{1,0:T(8,128)S(1)}, u32[]{:S(2)}, u32[]{:S(2)}) collective-permute-start(f32[96,256]{1,0:T(8,128)S(1)} %collective-permute-done.5.refs_7_), channel_id=1, source_target_pairs={{0,8},{8,0},{1,9},{9,1},{2,10},{10,2},{3,11},{11,3},{4,12},{12,4},... | collective-permute-start | bytes 294920 | tf_op jit(solution)/shard_map/ppermute | solution.py:24
  14.5 1.3 %collective-permute-start.8 = (f32[96,256]{1,0:T(8,128)S(1)}, f32[96,256]{1,0:T(8,128)S(1)}, u32[]{:S(2)}, u32[]{:S(2)}) collective-permute-start(f32[96,256]{1,0:T(8,128)S(1)} %collective-permute-done.7.refs_9_), channel_id=1, source_target_pairs={{0,8},{8,0},{1,9},{9,1},{2,10},{10,2},{3,11},{11,3},{4,12},{12,4},... | collective-permute-start | bytes 294920 | tf_op jit(solution)/shard_map/ppermute | solution.py:24
  17.7 5.1 %collective-permute-start.10 = (f32[96,128]{1,0:T(8,128)S(1)}, f32[96,128]{1,0:T(8,128)S(1)}, u32[]{:S(2)}, u32[]{:S(2)}) collective-permute-start(f32[96,128]{1,0:T(8,128)S(1)} %get-tuple-element.11), channel_id=1, source_target_pairs={{17,0},{16,1},{1,16},{0,17},{19,2},{18,3},{3,18},{2,19},{21,4},{20... | collective-permute-start | bytes 147464 | tf_op jit(solution)/shard_map/ppermute | solution.py:24
  19.2 4.3 %collective-permute-start.11 = (f32[96,128]{1,0:T(8,128)S(1)}, f32[96,128]{1,0:T(8,128)S(1)}, u32[]{:S(2)}, u32[]{:S(2)}) collective-permute-start(f32[96,128]{1,0:T(8,128)S(1)} %get-tuple-element.12), channel_id=1, source_target_pairs={{16,0},{17,1},{0,16},{1,17},{18,2},{19,3},{2,18},{3,19},{20,4},{21... | collective-permute-start | bytes 147464 | tf_op jit(solution)/shard_map/ppermute | solution.py:24
  19.7 4.1 %collective-permute-start.9 = (f32[96,128]{1,0:T(8,128)S(1)}, f32[96,128]{1,0:T(8,128)S(1)}, u32[]{:S(2)}, u32[]{:S(2)}) collective-permute-start(f32[96,128]{1,0:T(8,128)S(1)} %get-tuple-element.10), channel_id=1, source_target_pairs={{1,0},{0,1},{17,16},{16,17},{3,2},{2,3},{19,18},{18,19},{5,4},{4,5... | collective-permute-start | bytes 147464 | tf_op jit(solution)/shard_map/ppermute | solution.py:24

commit v4 on v3

--- a/solution.py
+++ b/solution.py
@@ -33,10 +33,10 @@
     return parts
 
 
-def product(left, right, dims):
-    terms = [(left[i], right[order - i]) for order in range(len(left)) for i in range(order + 1)]
-    long_left, long_right = (jnp.concatenate(side, axis=axis[0]) for side, axis in zip(zip(*terms), dims[0]))
-    return lax.dot_general(long_left, long_right, dims, preferred_element_type=jnp.float32)
+def product(left, right):
+    long_left = jnp.concatenate([part for part in left for _ in right], axis=1)
+    long_right = jnp.concatenate([part for _ in left for part in right], axis=1)
+    return lax.dot_general(long_left, long_right, NT, preferred_element_type=jnp.float32)
 
 
 def pack(features_ref, solves_ref, probes_ref, out_ref, both, sems):
@@ -77,15 +77,15 @@
     xs, ws = source[:, :features], source[:, features:]
     half = ws.shape[1] // 2
     ws = jnp.concatenate([ws[:, half:], ws[:, :half]], axis=1)
-    xs_pieces = pieces(xs, 3)
+    xs_pieces = pieces(xs, 2)
     square_t = jnp.sum(xt * xt, axis=1, keepdims=True)
     ones = jnp.ones((8, features), jnp.bfloat16)
     squares = [lax.dot_general(ones, part, NT, preferred_element_type=jnp.float32) for part in reversed(pieces(xs * xs, 3))]
-    inner = product(pieces(xt, 3), xs_pieces, NT)
+    inner = product(pieces(xt, 2), xs_pieces)
     kernel = jnp.exp(inner - (0.5 * square_t + 0.5 * sum(squares)[:1]))
-    coupling = kernel * product(pieces(wt, 2), pieces(ws, 2), NT)
+    coupling = kernel * product(pieces(wt, 2), pieces(ws, 2))
     totals = jnp.sum(coupling, axis=1, keepdims=True)
-    upper, lower = xs_pieces[:2]
+    upper, lower = xs_pieces
     right = jnp.concatenate(
         [jnp.concatenate([upper, lower], axis=1), jnp.concatenate([upper, jnp.zeros_like(lower)], axis=1)], axis=0
     )

time: 24.6 us -> 24.5 us (level)
  no operation moved by 1% of the time
where the time goes in v4:
time: 24.5 us; the launch traced here: 24.4 us
  starting transfers between devices  13 us (53%)
  waiting for transfers between devices  8.02 us (33%)
  Pallas kernels  2.62 us (11%)
  other arithmetic  0.65 us (3%)
    ppermute x12, starting transfers between devices, send(): lax.ppermute(block, axes, [(j, i) for i, j in pairs] if back else pairs)  13 us
    ppermute x12, waiting for transfers between devices, send(): lax.ppermute(block, axes, [(j, i) for i, j in pairs] if back else pairs)  8.02 us
    pallas_call x1, Pallas kernels, partial(): pl.pallas_call(functools.partial(couple, features, scale, (len(targets),...  1.72 us
    pallas_call x1, Pallas kernels, packed(): pl.pallas_call(pack, out_shape=pltpu.VMEM((rows, width), jnp.float32), in...  0.89 us
    add x1, other arithmetic, local(): out = out + part  0.64 us
  transfers between devices with their start and end apart: 12, of which 6 were waited for; matrix products, arithmetic and copies ran while one was open for 0% of the time, Pallas kernels for 0%

profile of v4, /device:TPU:0, one launch (start us, length us, event | category | flops | bytes accessed | tf_op | source)
XLA Modules:
  0.0 24.4 jit_solution(15771858893143518548)
XLA Ops:
  0.0 0.9 %shard_map.37.refs_0_.refs_3_ = f32[96,256]{1,0:T(8,128)S(1)} custom-call(f32[96,128]{1,0:T(8,128)} %features_ref.1, f32[64,96]{1,0:T(8,128)} %bitcast.2, f32[64,96]{1,0:T(8,128)} %bitcast.3), custom_call_target="tpu_custom_call" | custom-call | tf_op jit(solution)/shard_map/pallas_call | solution.py:59
  0.9 3.0 %collective-permute-start = (f32[96,256]{1,0:T(8,128)S(1)}, f32[96,256]{1,0:T(8,128)S(1)}, u32[]{:S(2)}, u32[]{:S(2)}) collective-permute-start(f32[96,256]{1,0:T(8,128)S(1)} %shard_map.37.refs_0_.refs_3_), channel_id=1, source_target_pairs={{0,1},{1,0},{2,3},{3,2},{4,5},{5,4},{6,7},{7,6},{8,9},{9,8},{10,11... | collective-permute-start | bytes 294920 | tf_op jit(solution)/shard_map/ppermute | solution.py:24
  3.9 2.6 %collective-permute-start.3 = (f32[96,256]{1,0:T(8,128)S(1)}, f32[96,256]{1,0:T(8,128)S(1)}, u32[]{:S(2)}, u32[]{:S(2)}) collective-permute-start(f32[96,256]{1,0:T(8,128)S(1)} %shard_map.37.refs_0_.refs_3_), channel_id=1, source_target_pairs={{0,4},{2,6},{4,0},{6,2},{1,5},{3,7},{5,1},{7,3},{8,12},{10,14},{12... | collective-permute-start | bytes 294920 | tf_op jit(solution)/shard_map/ppermute | solution.py:24
  6.5 1.6 %collective-permute-start.5 = (f32[96,256]{1,0:T(8,128)S(1)}, f32[96,256]{1,0:T(8,128)S(1)}, u32[]{:S(2)}, u32[]{:S(2)}) collective-permute-start(f32[96,256]{1,0:T(8,128)S(1)} %shard_map.37.refs_0_.refs_3_), channel_id=1, source_target_pairs={{0,2},{2,0},{4,6},{6,4},{1,3},{3,1},{5,7},{7,5},{8,10},{10,8},{12,... | collective-permute-start | bytes 294920 | tf_op jit(solution)/shard_map/ppermute | solution.py:24
  8.1 0.2 collective-permute-start.7
  8.3 0.0 collective-permute-done.refs_1_
  8.3 1.6 %collective-permute-start.1 = (f32[192,256]{1,0:T(8,128)S(1)}, f32[192,256]{1,0:T(8,128)S(1)}, u32[]{:S(2)}, u32[]{:S(2)}) collective-permute-start(f32[192,256]{1,0:T(8,128)S(1)} %pad_maximum_fusion), channel_id=1, source_target_pairs={{0,16},{16,0},{1,17},{17,1},{2,18},{18,2},{3,19},{19,3},{4,20},{20... | collective-permute-start | bytes 589832 | tf_op jit(solution)/shard_map/ppermute | solution.py:24
  9.9 0.0 collective-permute-start.2
  9.9 2.1 %collective-permute-done.3.refs_5_ = f32[96,256]{1,0:T(8,128)S(1)} collective-permute-done((f32[96,256]{1,0:T(8,128)S(1)}, f32[96,256]{1,0:T(8,128)S(1)}, u32[]{:S(2)}, u32[]{:S(2)}) %collective-permute-start.3) | collective-permute-done | bytes 98336 | tf_op jit(solution)/shard_map/ppermute | solution.py:24
  12.0 0.0 collective-permute-start.4
  12.0 0.0 collective-permute-done.5.refs_7_
  12.0 0.5 %collective-permute-start.6 = (f32[96,256]{1,0:T(8,128)S(1)}, f32[96,256]{1,0:T(8,128)S(1)}, u32[]{:S(2)}, u32[]{:S(2)}) collective-permute-start(f32[96,256]{1,0:T(8,128)S(1)} %collective-permute-done.5.refs_7_), channel_id=1, source_target_pairs={{0,8},{8,0},{1,9},{9,1},{2,10},{10,2},{3,11},{11,3},{4,12},{12,4},... | collective-permute-start | bytes 294920 | tf_op jit(solution)/shard_map/ppermute | solution.py:24
  12.5 2.0 %collective-permute-done.7.refs_9_ = f32[96,256]{1,0:T(8,128)S(1)} collective-permute-done((f32[96,256]{1,0:T(8,128)S(1)}, f32[96,256]{1,0:T(8,128)S(1)}, u32[]{:S(2)}, u32[]{:S(2)}) %collective-permute-start.7) | collective-permute-done | bytes 98336 | tf_op jit(solution)/shard_map/ppermute | solution.py:24
  14.5 0.0 collective-permute-start.8
  14.5 0.0 collective-permute-done.2.refs_4_
  14.6 0.0 collective-permute-done.4.refs_6_
  14.6 0.0 collective-permute-done.6.refs_8_
  14.6 1.3 %collective-permute-done.8.refs_10_ = f32[96,256]{1,0:T(8,128)S(1)} collective-permute-done((f32[96,256]{1,0:T(8,128)S(1)}, f32[96,256]{1,0:T(8,128)S(1)}, u32[]{:S(2)}, u32[]{:S(2)}) %collective-permute-start.8) | collective-permute-done | bytes 98336 | tf_op jit(solution)/shard_map/ppermute | solution.py:24
  15.8 0.0 collective-permute-done.1.refs_2_
  15.8 1.7 %shard_map.38 = (f32[96,128]{1,0:T(8,128)S(1)}, f32[96,128]{1,0:T(8,128)S(1)}, f32[96,128]{1,0:T(8,128)S(1)}, f32[96,128]{1,0:T(8,128)S(1)}) custom-call(f32[96,256]{1,0:T(8,128)S(1)} %shard_map.37.refs_0_.refs_3_, f32[96,256]{1,0:T(8,128)S(1)} %collective-permute-done.refs_1_, f32[192,256]{1,0:T(8,128)S(1)} %collective-permute-done.1.refs_2_, ...), custom_call_target="tpu_custom_call" | custom-call | flops 905969664 | bytes 1179648 | tf_op jit(solution)/shard_map/pallas_call | solution.py:102
  17.6 1.6 %collective-permute-start.10 = (f32[96,128]{1,0:T(8,128)S(1)}, f32[96,128]{1,0:T(8,128)S(1)}, u32[]{:S(2)}, u32[]{:S(2)}) collective-permute-start(f32[96,128]{1,0:T(8,128)S(1)} %get-tuple-element.11), channel_id=1, source_target_pairs={{17,0},{16,1},{1,16},{0,17},{19,2},{18,3},{3,18},{2,19},{21,4},{20... | collective-permute-start | bytes 147464 | tf_op jit(solution)/shard_map/ppermute | solution.py:24
  19.1 0.5 %collective-permute-start.11 = (f32[96,128]{1,0:T(8,128)S(1)}, f32[96,128]{1,0:T(8,128)S(1)}, u32[]{:S(2)}, u32[]{:S(2)}) collective-permute-start(f32[96,128]{1,0:T(8,128)S(1)} %get-tuple-element.12), channel_id=1, source_target_pairs={{16,0},{17,1},{0,16},{1,17},{18,2},{19,3},{2,18},{3,19},{20,4},{21... | collective-permute-start | bytes 147464 | tf_op jit(solution)/shard_map/ppermute | solution.py:24
  19.6 1.5 %collective-permute-start.9 = (f32[96,128]{1,0:T(8,128)S(1)}, f32[96,128]{1,0:T(8,128)S(1)}, u32[]{:S(2)}, u32[]{:S(2)}) collective-permute-start(f32[96,128]{1,0:T(8,128)S(1)} %get-tuple-element.10), channel_id=1, source_target_pairs={{1,0},{0,1},{17,16},{16,17},{3,2},{2,3},{19,18},{18,19},{5,4},{4,5... | collective-permute-start | bytes 147464 | tf_op jit(solution)/shard_map/ppermute | solution.py:24
  21.1 1.6 %collective-permute-done.10 = f32[96,128]{1,0:T(8,128)S(1)} collective-permute-done((f32[96,128]{1,0:T(8,128)S(1)}, f32[96,128]{1,0:T(8,128)S(1)}, u32[]{:S(2)}, u32[]{:S(2)}) %collective-permute-start.10) | collective-permute-done | bytes 49184 | tf_op jit(solution)/shard_map/ppermute | solution.py:24
  22.7 0.7 %collective-permute-done.11 = f32[96,128]{1,0:T(8,128)S(1)} collective-permute-done((f32[96,128]{1,0:T(8,128)S(1)}, f32[96,128]{1,0:T(8,128)S(1)}, u32[]{:S(2)}, u32[]{:S(2)}) %collective-permute-start.11) | collective-permute-done | bytes 49184 | tf_op jit(solution)/shard_map/ppermute | solution.py:24
  23.4 0.3 %collective-permute-done.9 = f32[96,128]{1,0:T(8,128)S(1)} collective-permute-done((f32[96,128]{1,0:T(8,128)S(1)}, f32[96,128]{1,0:T(8,128)S(1)}, u32[]{:S(2)}, u32[]{:S(2)}) %collective-permute-start.9) | collective-permute-done | bytes 49184 | tf_op jit(solution)/shard_map/ppermute | solution.py:24
  23.7 0.6 %add_add_fusion = f32[96,128]{1,0:T(8,128)} fusion(f32[96,128]{1,0:T(8,128)S(1)} %collective-permute-done.11, f32[96,128]{1,0:T(8,128)S(1)} %collective-permute-done.10, f32[96,128]{1,0:T(8,128)S(1)} %get-tuple-element.9, f32[96,128]{1,0:T(8,128)S(1)} %collective-permute-done.9), kind=kLoop, calls=%fused_computation.1 | loop fusion | flops 36864 | bytes 245760 | tf_op jit(solution)/shard_map/add | solution.py:137
  (1 shorter events, 0.0 us)
Async XLA Ops:
  0.9 7.4 %collective-permute-start = (f32[96,256]{1,0:T(8,128)S(1)}, f32[96,256]{1,0:T(8,128)S(1)}, u32[]{:S(2)}, u32[]{:S(2)}) collective-permute-start(f32[96,256]{1,0:T(8,128)S(1)} %shard_map.37.refs_0_.refs_3_), channel_id=1, source_target_pairs={{0,1},{1,0},{2,3},{3,2},{4,5},{5,4},{6,7},{7,6},{8,9},{9,8},{10,11... | collective-permute-start | bytes 294920 | tf_op jit(solution)/shard_map/ppermute | solution.py:24
  3.9 8.1 %collective-permute-start.3 = (f32[96,256]{1,0:T(8,128)S(1)}, f32[96,256]{1,0:T(8,128)S(1)}, u32[]{:S(2)}, u32[]{:S(2)}) collective-permute-start(f32[96,256]{1,0:T(8,128)S(1)} %shard_map.37.refs_0_.refs_3_), channel_id=1, source_target_pairs={{0,4},{2,6},{4,0},{6,2},{1,5},{3,7},{5,1},{7,3},{8,12},{10,14},{12... | collective-permute-start | bytes 294920 | tf_op jit(solution)/shard_map/ppermute | solution.py:24
  6.5 5.5 %collective-permute-start.5 = (f32[96,256]{1,0:T(8,128)S(1)}, f32[96,256]{1,0:T(8,128)S(1)}, u32[]{:S(2)}, u32[]{:S(2)}) collective-permute-start(f32[96,256]{1,0:T(8,128)S(1)} %shard_map.37.refs_0_.refs_3_), channel_id=1, source_target_pairs={{0,2},{2,0},{4,6},{6,4},{1,3},{3,1},{5,7},{7,5},{8,10},{10,8},{12,... | collective-permute-start | bytes 294920 | tf_op jit(solution)/shard_map/ppermute | solution.py:24
  8.1 6.5 %collective-permute-start.7 = (f32[96,256]{1,0:T(8,128)S(1)}, f32[96,256]{1,0:T(8,128)S(1)}, u32[]{:S(2)}, u32[]{:S(2)}) collective-permute-start(f32[96,256]{1,0:T(8,128)S(1)} %shard_map.37.refs_0_.refs_3_), channel_id=1, source_target_pairs={{0,6},{2,4},{4,2},{6,0},{1,7},{3,5},{5,3},{7,1},{8,14},{10,12},{12... | collective-permute-start | bytes 294920 | tf_op jit(solution)/shard_map/ppermute | solution.py:24
  8.3 7.5 %collective-permute-start.1 = (f32[192,256]{1,0:T(8,128)S(1)}, f32[192,256]{1,0:T(8,128)S(1)}, u32[]{:S(2)}, u32[]{:S(2)}) collective-permute-start(f32[192,256]{1,0:T(8,128)S(1)} %pad_maximum_fusion), channel_id=1, source_target_pairs={{0,16},{16,0},{1,17},{17,1},{2,18},{18,2},{3,19},{19,3},{4,20},{20... | collective-permute-start | bytes 589832 | tf_op jit(solution)/shard_map/ppermute | solution.py:24
  9.9 4.7 %collective-permute-start.2 = (f32[96,256]{1,0:T(8,128)S(1)}, f32[96,256]{1,0:T(8,128)S(1)}, u32[]{:S(2)}, u32[]{:S(2)}) collective-permute-start(f32[96,256]{1,0:T(8,128)S(1)} %shard_map.37.refs_0_.refs_3_), channel_id=1, source_target_pairs={{0,8},{8,0},{1,9},{9,1},{2,10},{10,2},{3,11},{11,3},{4,12},{12,4},... | collective-permute-start | bytes 294920 | tf_op jit(solution)/shard_map/ppermute | solution.py:24
  12.0 2.6 %collective-permute-start.4 = (f32[96,256]{1,0:T(8,128)S(1)}, f32[96,256]{1,0:T(8,128)S(1)}, u32[]{:S(2)}, u32[]{:S(2)}) collective-permute-start(f32[96,256]{1,0:T(8,128)S(1)} %collective-permute-done.3.refs_5_), channel_id=1, source_target_pairs={{0,8},{8,0},{1,9},{9,1},{2,10},{10,2},{3,11},{11,3},{4,12},{12,4},... | collective-permute-start | bytes 294920 | tf_op jit(solution)/shard_map/ppermute | solution.py:24
  12.0 2.6 %collective-permute-start.6 = (f32[96,256]{1,0:T(8,128)S(1)}, f32[96,256]{1,0:T(8,128)S(1)}, u32[]{:S(2)}, u32[]{:S(2)}) collective-permute-start(f32[96,256]{1,0:T(8,128)S(1)} %collective-permute-done.5.refs_7_), channel_id=1, source_target_pairs={{0,8},{8,0},{1,9},{9,1},{2,10},{10,2},{3,11},{11,3},{4,12},{12,4},... | collective-permute-start | bytes 294920 | tf_op jit(solution)/shard_map/ppermute | solution.py:24
  14.5 1.3 %collective-permute-start.8 = (f32[96,256]{1,0:T(8,128)S(1)}, f32[96,256]{1,0:T(8,128)S(1)}, u32[]{:S(2)}, u32[]{:S(2)}) collective-permute-start(f32[96,256]{1,0:T(8,128)S(1)} %collective-permute-done.7.refs_9_), channel_id=1, source_target_pairs={{0,8},{8,0},{1,9},{9,1},{2,10},{10,2},{3,11},{11,3},{4,12},{12,4},... | collective-permute-start | bytes 294920 | tf_op jit(solution)/shard_map/ppermute | solution.py:24
  17.6 5.1 %collective-permute-start.10 = (f32[96,128]{1,0:T(8,128)S(1)}, f32[96,128]{1,0:T(8,128)S(1)}, u32[]{:S(2)}, u32[]{:S(2)}) collective-permute-start(f32[96,128]{1,0:T(8,128)S(1)} %get-tuple-element.11), channel_id=1, source_target_pairs={{17,0},{16,1},{1,16},{0,17},{19,2},{18,3},{3,18},{2,19},{21,4},{20... | collective-permute-start | bytes 147464 | tf_op jit(solution)/shard_map/ppermute | solution.py:24
  19.1 4.3 %collective-permute-start.11 = (f32[96,128]{1,0:T(8,128)S(1)}, f32[96,128]{1,0:T(8,128)S(1)}, u32[]{:S(2)}, u32[]{:S(2)}) collective-permute-start(f32[96,128]{1,0:T(8,128)S(1)} %get-tuple-element.12), channel_id=1, source_target_pairs={{16,0},{17,1},{0,16},{1,17},{18,2},{19,3},{2,18},{3,19},{20,4},{21... | collective-permute-start | bytes 147464 | tf_op jit(solution)/shard_map/ppermute | solution.py:24
  19.6 4.1 %collective-permute-start.9 = (f32[96,128]{1,0:T(8,128)S(1)}, f32[96,128]{1,0:T(8,128)S(1)}, u32[]{:S(2)}, u32[]{:S(2)}) collective-permute-start(f32[96,128]{1,0:T(8,128)S(1)} %get-tuple-element.10), channel_id=1, source_target_pairs={{1,0},{0,1},{17,16},{16,17},{3,2},{2,3},{19,18},{18,19},{5,4},{4,5... | collective-permute-start | bytes 147464 | tf_op jit(solution)/shard_map/ppermute | solution.py:24
